TPU v7x, 128 devices: a whole 4x4x4 slice. The times are simulated.
128 devices in a mesh: tm: 16 (over z, x_lo, core), lat: 8 (over x_hi, y).
Axes of the slice: x: 4 (x_hi: 2, x_lo: 2; x = x_hi * 2 + x_lo), y: 4, z: 4, core: 2. Of those that a mesh axis runs over, the one named last changes fastest.
Arguments:
- field: bfloat16 [2560, 192, 360], P('tm', 'lat'), may hold values from -6 to 6
- time_factor: bfloat16 [2560, 2560], replicated, may hold values from -2 to 2
- lat_factor: bfloat16 [192, 192], replicated, may hold values from -2 to 2
- lon_factor: bfloat16 [360, 360], replicated, may hold values from -2 to 2
Outputs:
- weights: bfloat16 [2560, 69120], P(None, ('tm', 'lat'))
All inputs are finite; a program needn't handle non-finite values.
Results may differ from a plain program's by a relative error of at most 0.0057.
Values may be sent and summed in bfloat16 or wider, within the bound.
No kernel may reach another device: no remote copies, remote signals or barrier semaphores. Data moves between devices by JAX's collectives and lax.ppermute only.
A program may use at most 64 MiB of HBM per device.

v0:
```python
import jax
import jax.numpy as jnp
from jax import lax
from jax.sharding import PartitionSpec as P


def on_device(field, time_factor, lat_factor, lon_factor):
    hours, rows, columns = field.shape
    first = jnp.dot(
        field.reshape(hours * rows, columns), lon_factor, preferred_element_type=jnp.float32
    )
    first = first.astype(jnp.bfloat16).reshape(hours, rows, columns)
    mixed = jnp.einsum(
        "im,tmj->tij",
        lat_factor,
        lax.all_to_all(first, "lat", split_axis=0, concat_axis=1, tiled=True),
        preferred_element_type=jnp.float32,
    )
    second = mixed.astype(jnp.bfloat16)
    few_hours = second.shape[0]
    second = second.reshape(few_hours, second.shape[1] * second.shape[2])
    gathered = lax.all_to_all(second, ("tm", "lat"), split_axis=1, concat_axis=0, tiled=True)
    weights = jnp.dot(time_factor, gathered, preferred_element_type=jnp.float32)
    return weights.astype(jnp.bfloat16)


def solution(mesh):
    return jax.shard_map(
        on_device,
        mesh=mesh,
        in_specs=(P("tm", "lat", None), P(), P(), P()),
        out_specs=P(None, ("tm", "lat")),
        check_vma=False,
    )
```

profile of v0, /device:TPU:1, one launch (start us, length us, event | category | flops | bytes accessed | tf_op | source)
XLA Modules:
  0.0 146.0 jit_solution(12798195945316848385)
XLA Ops:
  0.0 0.0 copy-start
  0.0 1.8 %copy-done = bf16[160,24,360]{2,1,0:T(8,128)(2,1)S(1)} copy-done((bf16[160,24,360]{2,1,0:T(8,128)(2,1)S(1)}, bf16[160,24,360]{2,1,0:T(8,128)(2,1)}, u32[]{:S(2)}) %copy-start) | copy-done | bytes 2764824
  1.8 4.1 %convolution_convert_fusion = bf16[3840,360]{0,1:T(8,128)(2,1)} fusion(bf16[3840,360]{1,0:T(8,128)(2,1)S(1)} %bitcast.19, bf16[360,360]{1,0:T(8,128)(2,1)} %param.7), kind=kOutput, calls=%fused_computation | convolution fusion | flops 996710400 | bytes 5788800 | tf_op jit(solution)/shard_map/dot_general | solution.py:9
  6.0 4.5 %copy.9 = bf16[3840,360]{1,0:T(8,128)(2,1)} copy(bf16[3840,360]{0,1:T(8,128)(2,1)} %convolution_convert_fusion) | data formatting | bytes 5529600 | tf_op jit(solution)/shard_map/convert_element_type | solution.py:12
  10.4 43.8 %all_to_all.37 = bf16[160,24,360]{2,1,0:T(8,128)(2,1)S(1)} all-to-all(bf16[160,24,360]{2,1,0:T(8,128)(2,1)} %bitcast.21), channel_id=1, replica_groups=mesh['tm'=16,'lat'=8] {'lat'}, dimensions={0} | all-to-all | bytes 5529600 | tf_op jit(solution)/shard_map/all_to_all | solution.py:16
  54.2 0.0 copy-start.1
  54.2 0.5 copy.10
  54.7 0.4 copy-done.1
  55.1 2.5 %convert_bitcast_fusion = bf16[20,192,360]{2,1,0:T(8,128)(2,1)} fusion(bf16[20,192,360]{2,1,0:T(8,128)(2,1)S(1)} %bitcast.23, bf16[192,192]{1,0:T(8,128)(2,1)S(1)} %copy-done.1), kind=kOutput, calls=%fused_computation.3 | convolution fusion | flops 532224000 | bytes 5603328 | tf_op jit(solution)/shard_map/im,tmj->tij/dot_general | solution.py:13
  57.6 7.4 %all_to_all.31 = bf16[20,128,540]{2,1,0:T(8,128)(2,1)} reshape(bf16[20,192,360]{2,1,0:T(8,128)(2,1)} %convert_bitcast_fusion) | data formatting | bytes 5529600 | tf_op jit(solution)/shard_map/all_to_all | solution.py:22
  65.1 3.8 %copy.11 = bf16[20,128,540]{2,0,1:T(8,128)(2,1)S(1)} copy(bf16[20,128,540]{2,1,0:T(8,128)(2,1)} %all_to_all.31) | data formatting | bytes 5529600 | tf_op jit(solution)/shard_map/all_to_all | solution.py:22
  68.9 56.6 %all_to_all.38 = bf16[20,128,540]{2,0,1:T(8,128)(2,1)} all-to-all(bf16[20,128,540]{2,0,1:T(8,128)(2,1)S(1)} %copy.11), channel_id=1, replica_groups=mesh['tm'=16,'lat'=8] {'tm','lat'}, dimensions={1} | all-to-all | bytes 5529600 | tf_op jit(solution)/shard_map/all_to_all | solution.py:22
  125.5 6.6 %all_to_all.34 = bf16[2560,540]{1,0:T(8,128)(2,1)} reshape(bf16[128,20,540]{2,1,0:T(8,128)(2,1)} %bitcast.20) | data formatting | bytes 5529600 | tf_op jit(solution)/shard_map/all_to_all | solution.py:22
  132.1 14.0 %fusion = bf16[2560,540]{0,1:T(8,128)(2,1)} fusion(bf16[2560,540]{1,0:T(8,128)(2,1)} %all_to_all.34, bf16[2560,2560]{1,0:T(8,128)(2,1)} %param.5), kind=kOutput, calls=%fused_computation.2 | convolution fusion | flops 7079270400 | bytes 18636800 | tf_op jit(solution)/shard_map/dot_general | solution.py:23
Async XLA Ops:
  0.0 1.8 %copy-start = (bf16[160,24,360]{2,1,0:T(8,128)(2,1)S(1)}, bf16[160,24,360]{2,1,0:T(8,128)(2,1)}, u32[]{:S(2)}) copy-start(bf16[160,24,360]{2,1,0:T(8,128)(2,1)} %param.4) | copy-start | bytes 8294404
  54.2 0.9 copy-start.1
where the time goes:
time: 148 us; the launch traced here: 146 us
  blocking collectives  100 us (68%)
  local copies, waits for them, and re-layouts  25 us (17%)
  matrix products  20.6 us (14%)
    all_to_all x1, blocking collectives, on_device(): lax.all_to_all(second, ('tm', 'lat'), split_axis=1, concat_axis=0, tiled=...  56.6 us
    all_to_all x1, blocking collectives, on_device(): lax.all_to_all(first, 'lat', split_axis=0, concat_axis=1, tiled=True)  43.8 us
    all_to_all x3, local copies, waits for them, and re-layouts, on_device(): lax.all_to_all(second, ('tm', 'lat'), split_axis=1, concat_axis=0, tiled=...  17.9 us
    dot_general x1, matrix products, on_device(): weights = jnp.dot(time_factor, gathered, preferred_element_type=jnp.float32)  14 us
    convert_element_type x1, local copies, waits for them, and re-layouts, on_device(): first = first.astype(jnp.bfloat16).reshape(hours, rows, columns)  4.46 us
    dot_general x1, matrix products, on_device(): jnp.dot(field.reshape(hours * rows, columns), lon_factor, preferred_eleme...  4.14 us

commit v1 on v0

v1 whole, which is shorter than its diff:
```python
import functools

import jax
import jax.numpy as jnp
from jax import lax
from jax.experimental import pallas as pl
from jax.experimental.pallas import tpu as pltpu
from jax.sharding import PartitionSpec as P

LANES = 128
CELLS = 540
BLOCK = 88
VMEM = 60 * 1024 * 1024


def mix_kernel(x_ref, lon_ref, lat_ref, out_ref, first_ref, second_ref):
    parts, hours, few, columns = x_ref.shape
    rows = parts * few
    third = rows // 3
    lon = lon_ref[...]
    for part in range(parts):
        x = x_ref[part].astype(jnp.float32).reshape(hours * few, columns).astype(jnp.bfloat16)
        first = jnp.dot(x, lon, preferred_element_type=jnp.float32)
        first_ref[part] = first.astype(jnp.bfloat16).astype(jnp.float32).reshape(hours, few, columns)
    lat = lat_ref[...]

    def hour(t, carry):
        f = first_ref[:, t].reshape(rows, columns).astype(jnp.bfloat16)
        s = jnp.dot(lat, f, preferred_element_type=jnp.float32)
        for k in range(3):
            width = min(LANES, columns - LANES * k)
            second_ref[k, pl.ds(t * rows, rows), :width] = s[:, LANES * k : LANES * k + width]
        return carry

    lax.fori_loop(0, hours, hour, 0)
    lane = lax.broadcasted_iota(jnp.int32, (24, LANES), 1)
    low = lax.broadcasted_iota(jnp.int32, (8, LANES), 0) < 4
    narrow = lane[:8] < 32

    def tile(v, k):
        return v[:, LANES * k : LANES * (k + 1)]

    def pack(tiles):
        body = [t[:16] for t in tiles[:4]]
        tails = [t[16:24] for t in tiles[:4]]
        for k in (0, 2):
            body.append(jnp.where(low, tails[k], pltpu.roll(tails[k + 1], 4, 0)))
        rest = tiles[4]
        last = jnp.where(
            narrow,
            rest[:8],
            jnp.where(lane[:8] < 64, pltpu.roll(rest[8:16], 32, 1), pltpu.roll(rest[16:24], 64, 1)),
        )
        body.append(last)
        return jnp.concatenate(body, axis=0).astype(jnp.bfloat16)

    def triple(p, carry):
        a, b, c = (
            jnp.concatenate([second_ref[jnp.int32(k), pl.ds(jnp.int32(r * third) + p, 24, rows), :] for k in range(3)], axis=1)
            for r in range(3)
        )
        b_up = pltpu.roll(b, 104, 1)
        out_ref[2 * p] = pack(
            [
                tile(a, 0),
                tile(a, 1),
                jnp.where(lane < 104, tile(a, 2), tile(b_up, 0)),
                tile(b_up, 1),
                tile(b_up, 2),
            ]
        )
        b_down = pltpu.roll(b, 204, 1)
        c_up = pltpu.roll(c, 180, 1)
        out_ref[2 * p + 1] = pack(
            [
                tile(b_down, 0),
                jnp.where(lane < 52, tile(b_down, 1), tile(c_up, 1)),
                tile(c_up, 2),
                tile(c_up, 0),
                tile(c_up, 1),
            ]
        )
        return carry

    lax.fori_loop(0, third, triple, 0)


def mix(x, lon, lat):
    parts, hours, few, columns = x.shape
    rows = parts * few
    return pl.pallas_call(
        mix_kernel,
        out_shape=jax.ShapeDtypeStruct((2 * rows // 3, BLOCK, LANES), jnp.bfloat16),
        scratch_shapes=[
            pltpu.VMEM((parts, hours, few, columns), jnp.float32),
            pltpu.VMEM((3, 24 * rows, LANES), jnp.float32),
        ],
        compiler_params=pltpu.CompilerParams(vmem_limit_bytes=VMEM),
    )(x, lon, lat)


def time_kernel(r_ref, t_ref, out_ref, g_ref, gt_ref):
    sources = r_ref.shape[0]
    total = gt_ref.shape[1]

    @pl.when(pl.program_id(0) == 0)
    def _():
        low = lax.broadcasted_iota(jnp.int32, (8, LANES), 0) < 4

        def pieces(r, k):
            if k == 4:
                last = r[80:88]
                return last, pltpu.roll(last, 96, 1), pltpu.roll(last, 64, 1), False
            tail = 64 + 8 * (k // 2)
            return r[16 * k : 16 * k + 8], r[16 * k + 8 : 16 * k + 16], r[tail : tail + 8], k % 2 == 1

        def unpack(pair, carry):
            r0 = r_ref[2 * pair].astype(jnp.float32)
            r1 = r_ref[2 * pair + 1].astype(jnp.float32)
            start = pl.multiple_of(pair * 40, 8)
            for k in range(5):
                a0, a1, a2, high = pieces(r0, k)
                b0, b1, b2, _ = pieces(r1, k)
                if high:
                    a2 = pltpu.roll(a2, 4, 0)
                else:
                    b2 = pltpu.roll(b2, 4, 0)
                b0, b1 = pltpu.roll(b0, 4, 0), pltpu.roll(b1, 4, 0)
                both = [a0, a1, jnp.where(low, a2, b0), jnp.where(low, b0, b1), jnp.where(low, b1, b2)]
                g_ref[pl.ds(start, 40), LANES * k : LANES * (k + 1)] = jnp.concatenate(both, axis=0)
            return carry

        lax.fori_loop(0, sources // 2, unpack, 0)
        for k in range(5):
            width = min(LANES, gt_ref.shape[0] - LANES * k)
            for h in range(0, total, 512):
                block = g_ref[h : h + 512, LANES * k : LANES * (k + 1)]
                gt_ref[LANES * k : LANES * k + width, h : h + 512] = block.T[:width].astype(jnp.bfloat16)

    w = lax.dot_general(
        gt_ref[...], t_ref[...], (((1,), (1,)), ((), ())), preferred_element_type=jnp.float32
    )
    out_ref[...] = w[:CELLS].astype(jnp.bfloat16)


def time_product(r, time_factor):
    few = 256
    total = time_factor.shape[1]
    return pl.pallas_call(
        time_kernel,
        grid=(time_factor.shape[0] // few,),
        in_specs=[
            pl.BlockSpec(r.shape, lambda i: (0, 0, 0)),
            pl.BlockSpec((few, total), lambda i: (i, 0)),
        ],
        out_specs=pl.BlockSpec((CELLS, few), lambda i: (0, i)),
        out_shape=jax.ShapeDtypeStruct((CELLS, time_factor.shape[0]), jnp.bfloat16),
        scratch_shapes=[
            pltpu.VMEM((total, 5 * LANES), jnp.float32),
            pltpu.VMEM((544, total), jnp.bfloat16),
        ],
        compiler_params=pltpu.CompilerParams(vmem_limit_bytes=VMEM),
    )(r, time_factor)


def on_device(field, time_factor, lat_factor, lon_factor):
    hours, few, columns = field.shape
    parts = lax.axis_size("lat")
    moved = lax.all_to_all(field, "lat", split_axis=0, concat_axis=0, tiled=True)
    moved = moved.reshape(parts, hours // parts, few, columns)
    rows = lat_factor.shape[0]
    lat = lat_factor.reshape(rows // 3, 3, rows).transpose(1, 0, 2).reshape(rows, rows)
    blocks = mix(moved, lon_factor, lat)
    gathered = lax.all_to_all(blocks, ("tm", "lat"), split_axis=0, concat_axis=0, tiled=True)
    return time_product(gathered, time_factor).T


def solution(mesh):
    return jax.shard_map(
        on_device,
        mesh=mesh,
        in_specs=(P("tm", "lat", None), P(), P(), P()),
        out_specs=P(None, ("tm", "lat")),
        check_vma=False,
    )
```

time: 148 us -> 134 us (0.905)
  blocking collectives: 100 us -> 46.6 us
  Pallas kernels: 0 us -> 41.7 us
  waiting for transfers between devices: 0 us -> 34.6 us
  local copies, waits for them, and re-layouts: 25 us -> 2.31 us
  matrix products: 20.6 us -> 0 us
  starting transfers between devices: 0 us -> 7.61 us
    all_to_all x2 -> x1, blocking collectives: 100 us -> 46.6 us  [on_device(): lax.all_to_all(blocks, ('tm', 'lat'), split_axis=0, concat_axis=0, tiled=...]
    pallas_call x0 -> x2, Pallas kernels: none -> 41.7 us  [the longest x1 21.3 us: mix(): pl.pallas_call(mix_kernel, out_shape=jax.ShapeDtypeStruct((2 * rows // 3,...]
    all_to_all x0 -> x1, waiting for transfers between devices: none -> 34.6 us  [on_device(): lax.all_to_all(field, 'lat', split_axis=0, concat_axis=0, tiled=True)]
    dot_general x3 -> x0, matrix products: 20.6 us -> none  [the longest x1 14 us: on_device(): weights = jnp.dot(time_factor, gathered, preferred_element_type=jnp.float32)]
    all_to_all x4 -> x0, local copies, waits for them, and re-layouts: 18.4 us -> none  [the longest x3 17.9 us: on_device(): lax.all_to_all(second, ('tm', 'lat'), split_axis=1, concat_axis=0, tiled=...]
    all_to_all x0 -> x1, starting transfers between devices: none -> 7.61 us  [on_device(): lax.all_to_all(field, 'lat', split_axis=0, concat_axis=0, tiled=True)]
    convert_element_type x1 -> x0, local copies, waits for them, and re-layouts: 4.46 us -> none  [on_device(): first = first.astype(jnp.bfloat16).reshape(hours, rows, columns)]
  transfers between devices with their start and end apart: 0 -> 1, of which waited for: 0 -> 1; matrix products, arithmetic and copies ran while one was open for 0% -> 1% of each run, Pallas kernels for 0% -> 0%
where the time goes in v1:
time: 134 us; the launch traced here: 133 us
  blocking collectives  46.6 us (35%)
  Pallas kernels  41.7 us (31%)
  waiting for transfers between devices  34.6 us (26%)
  starting transfers between devices  7.61 us (6%)
  local copies, waits for them, and re-layouts  2.31 us (2%)
    all_to_all x1, blocking collectives, on_device(): lax.all_to_all(blocks, ('tm', 'lat'), split_axis=0, concat_axis=0, tiled=...  46.6 us
    all_to_all x1, waiting for transfers between devices, on_device(): lax.all_to_all(field, 'lat', split_axis=0, concat_axis=0, tiled=True)  34.6 us
    pallas_call x1, Pallas kernels, mix(): pl.pallas_call(mix_kernel, out_shape=jax.ShapeDtypeStruct((2 * rows // 3,...  21.3 us
    pallas_call x1, Pallas kernels, time_product(): pl.pallas_call(time_kernel, grid=(time_factor.shape[0] // few,), in_specs...  20.4 us
    all_to_all x1, starting transfers between devices, on_device(): lax.all_to_all(field, 'lat', split_axis=0, concat_axis=0, tiled=True)  7.61 us
  transfers between devices with their start and end apart: 1, of which 1 were waited for; matrix products, arithmetic and copies ran while one was open for 1% of the time, Pallas kernels for 0%

profile of v1, /device:TPU:1, one launch (start us, length us, event | category | flops | bytes accessed | tf_op | source)
XLA Modules:
  0.0 132.8 jit_solution(10020119992142183835)
XLA Ops:
  0.0 0.0 copy-start.1
  0.0 7.6 %all-to-all-start = ((bf16[160,24,360]{2,1,0:T(8,128)(2,1)}), bf16[160,24,360]{2,1,0:T(8,128)(2,1)S(1)}, u32[]{:S(2)}, u32[]{:S(2)}) async-start(bf16[160,24,360]{2,1,0:T(8,128)(2,1)} %param.4), calls=%async_computation | async-start | bytes 5898240 | tf_op jit(solution)/shard_map/all_to_all | solution.py:169
  7.6 0.0 copy-done.1
  7.6 0.1 reshape.10
  7.7 0.7 copy.6
  8.3 34.6 %all-to-all-done = bf16[160,24,360]{2,1,0:T(8,128)(2,1)S(1)} async-done(((bf16[160,24,360]{2,1,0:T(8,128)(2,1)}), bf16[160,24,360]{2,1,0:T(8,128)(2,1)S(1)}, u32[]{:S(2)}, u32[]{:S(2)}) %all-to-all-start) | async-done | bytes 2764832 | tf_op jit(solution)/shard_map/all_to_all | solution.py:169
  42.9 0.0 copy-start
  42.9 1.6 %copy-done = bf16[160,24,360]{2,1,0:T(8,128)(2,1)} copy-done((bf16[160,24,360]{2,1,0:T(8,128)(2,1)}, bf16[160,24,360]{2,1,0:T(8,128)(2,1)S(1)}, u32[]{:S(2)}) %copy-start) | copy-done | bytes 2764824
  44.5 21.3 %shard_map.46 = bf16[128,88,128]{2,1,0:T(8,128)(2,1)} custom-call(bf16[8,20,24,360]{3,2,1,0:T(8,128)(2,1)} %bitcast.4, bf16[360,360]{1,0:T(8,128)(2,1)} %lon_ref.1, bf16[192,192]{1,0:T(8,128)(2,1)} %bitcast.6), custom_call_target="tpu_custom_call" | custom-call | tf_op jit(solution)/shard_map/pallas_call | solution.py:91
  65.8 46.6 %all_to_all.10.r_ref = bf16[128,88,128]{2,1,0:T(8,128)(2,1)} all-to-all(bf16[128,88,128]{2,1,0:T(8,128)(2,1)} %shard_map.46), channel_id=1, replica_groups=mesh['tm'=16,'lat'=8] {'tm','lat'}, dimensions={0} | all-to-all | bytes 5767168 | tf_op jit(solution)/shard_map/all_to_all | solution.py:174
  112.3 20.4 %shard_map.47 = bf16[540,2560]{1,0:T(8,128)(2,1)} custom-call(bf16[128,88,128]{2,1,0:T(8,128)(2,1)} %all_to_all.10.r_ref, bf16[2560,2560]{1,0:T(8,128)(2,1)} %t_ref.1), custom_call_target="tpu_custom_call" | custom-call | tf_op jit(solution)/shard_map/pallas_call | solution.py:149
Async XLA Ops:
  0.0 7.6 %copy-start.1 = (bf16[192,192]{1,0:T(8,128)(2,1)S(1)}, bf16[192,192]{1,0:T(8,128)(2,1)}, u32[]{:S(2)}) copy-start(bf16[192,192]{1,0:T(8,128)(2,1)} %param.6) | copy-start | bytes 221188
  0.0 42.9 %all-to-all-start = ((bf16[160,24,360]{2,1,0:T(8,128)(2,1)}), bf16[160,24,360]{2,1,0:T(8,128)(2,1)S(1)}, u32[]{:S(2)}, u32[]{:S(2)}) async-start(bf16[160,24,360]{2,1,0:T(8,128)(2,1)} %param.4), calls=%async_computation | async-start | bytes 5898240 | tf_op jit(solution)/shard_map/all_to_all | solution.py:169
  42.9 1.6 %copy-start = (bf16[160,24,360]{2,1,0:T(8,128)(2,1)}, bf16[160,24,360]{2,1,0:T(8,128)(2,1)S(1)}, u32[]{:S(2)}) copy-start(bf16[160,24,360]{2,1,0:T(8,128)(2,1)S(1)} %all-to-all-done) | copy-start | bytes 8294404

commit v2 on v0

v2 whole, which is shorter than its diff:
```python
import jax
import jax.numpy as jnp
from jax import lax
from jax.experimental import pallas as pl
from jax.experimental.pallas import tpu as pltpu
from jax.sharding import PartitionSpec as P

LANES = 128
CELLS = 540
TALL = 544
HOURS = 20
MAIN = 16
BLOCK = 88
GROUP = 32 * HOURS
STRIDE = 200
COPIES = 8
WHOLE = pl.BlockSpec(memory_space=pltpu.VMEM)
OUTSIDE = pl.BlockSpec(memory_space=pltpu.HBM)


def params(mib):
    return pltpu.CompilerParams(vmem_limit_bytes=mib * 1024 * 1024)


def tile(v, k):
    return v[:, LANES * k : LANES * (k + 1)]


def pack(tiles, row, lane):
    tails = [jnp.where(row < 4, tiles[k][16:], pltpu.roll(tiles[k + 1][16:], 4, 0)) for k in (0, 2)]
    rest = tiles[4]
    last = jnp.where(
        lane < 32,
        rest[:8],
        jnp.where(lane < 64, pltpu.roll(rest[8:16], 32, 1), pltpu.roll(rest[16:], 64, 1)),
    )
    return jnp.concatenate([t[:16] for t in tiles[:4]] + tails + [last], axis=0).astype(jnp.bfloat16)


def mix_kernel(x_ref, lon_ref, lat_ref, to_ref, first_ref, second_ref, out_ref, sem):
    parts, hours, few, columns = x_ref.shape
    rows = parts * few
    third = rows // 3
    lon = lon_ref[...]

    def part_of_first(part, carry):
        x = x_ref[part].astype(jnp.float32).reshape(hours * few, columns).astype(jnp.bfloat16)
        first = jnp.dot(x, lon, preferred_element_type=jnp.float32)
        first_ref[part] = first.reshape(hours, few, columns)
        return carry

    lax.fori_loop(0, parts, part_of_first, 0, unroll=4)
    lat = lat_ref[...]

    def hour(t, carry):
        f = first_ref[:, t].reshape(rows, columns).astype(jnp.bfloat16)
        s = jnp.dot(lat, f, preferred_element_type=jnp.float32)
        at = pl.ds(pl.multiple_of(t * STRIDE, 8), rows)
        for k in range(3):
            width = min(LANES, columns - LANES * k)
            second_ref[k, at, :width] = s[:, LANES * k : LANES * k + width]
        return carry

    lax.fori_loop(0, hours, hour, 0, unroll=10)
    row = lax.broadcasted_iota(jnp.int32, (8, LANES), 0)
    lane8 = lax.broadcasted_iota(jnp.int32, (8, LANES), 1)
    lane = lax.broadcasted_iota(jnp.int32, (24, LANES), 1)

    def triple(p, carry):
        a, b, c = (
            jnp.concatenate(
                [second_ref[jnp.int32(k), pl.ds(jnp.int32(r * third) + p, 24, STRIDE), :] for k in range(3)], axis=1
            )
            for r in range(3)
        )
        b_up = pltpu.roll(b, 104, 1)
        out_ref[2 * p] = pack(
            [tile(a, 0), tile(a, 1), jnp.where(lane < 104, tile(a, 2), tile(b_up, 0)), tile(b_up, 1), tile(b_up, 2)],
            row,
            lane8,
        )
        b_down = pltpu.roll(b, 204, 1)
        c_up = pltpu.roll(c, 180, 1)
        out_ref[2 * p + 1] = pack(
            [
                tile(b_down, 0),
                jnp.where(lane < 52, tile(b_down, 1), tile(c_up, 1)),
                tile(c_up, 2),
                tile(c_up, 0),
                tile(c_up, 1),
            ],
            row,
            lane8,
        )
        return carry

    each = out_ref.shape[0] // COPIES

    def leave(n):
        at = pl.ds(n * each, each)
        return pltpu.make_async_copy(out_ref.at[at], to_ref.at[at], sem.at[n])

    def some(n, carry):
        lax.fori_loop(0, each // 8, lambda q, c: [triple(n * (each // 2) + 4 * q + i, c) for i in range(4)][-1], 0)
        leave(n).start()
        return carry

    lax.fori_loop(0, COPIES, some, 0)
    for n in range(COPIES):
        leave(n).wait()


def mix(x, lon, lat):
    parts, hours, few, columns = x.shape
    rows = lat.shape[0]
    return pl.pallas_call(
        mix_kernel,
        in_specs=[WHOLE] * 3,
        out_specs=OUTSIDE,
        out_shape=jax.ShapeDtypeStruct((2 * rows // 3, BLOCK, LANES), jnp.bfloat16),
        scratch_shapes=[
            pltpu.VMEM((parts, hours, few, columns), jnp.float32),
            pltpu.VMEM((3, 24 * STRIDE, LANES), jnp.float32),
            pltpu.VMEM((2 * rows // 3, BLOCK, LANES), jnp.bfloat16),
            pltpu.SemaphoreType.DMA((COPIES,)),
        ],
        compiler_params=params(24),
    )(x, lon, lat)


def order_kernel(t_ref, move_ref, out_ref):
    move = move_ref[...]
    total = t_ref.shape[1]
    main = 32 * MAIN
    tail = GROUP - main
    for u in range(total // GROUP):
        w = jnp.dot(t_ref[:, GROUP * u : GROUP * (u + 1)], move, preferred_element_type=jnp.float32).astype(jnp.bfloat16)
        out_ref[:, main * u : main * (u + 1)] = w[:, :main]
        start = total // GROUP * main + tail * u
        out_ref[:, start : start + tail] = w[:, main:]


def order_columns(time_factor):
    rows, total = time_factor.shape
    col = jnp.arange(GROUP)
    main = 32 * MAIN
    hour = jnp.where(col < main, col // MAIN * HOURS + col % MAIN, (col - main) % 32 * HOURS + MAIN + (col - main) // 32)
    move = (jnp.arange(GROUP)[:, None] == hour[None, :]).astype(jnp.bfloat16)
    few = 256
    return pl.pallas_call(
        order_kernel,
        grid=(rows // few,),
        in_specs=[pl.BlockSpec((few, total), lambda i: (i, 0)), pl.BlockSpec((GROUP, GROUP), lambda i: (0, 0))],
        out_specs=pl.BlockSpec((few, total), lambda i: (i, 0)),
        out_shape=jax.ShapeDtypeStruct((rows, total), jnp.bfloat16),
        compiler_params=params(16),
    )(time_factor, move)


def unpack(r_ref, gt_ref, tail_ref):
    sources = r_ref.shape[0]
    main = sources * MAIN
    few = BLOCK - 64
    tail_ref[...] = r_ref[:, 64:].astype(jnp.float32).reshape(sources * few, LANES)

    def tails(first):
        parts = []
        for u in range(sources // 32):
            for i in range(HOURS - MAIN):
                parts.append(tail_ref[pl.ds(u * 32 * few + first + i, 32, few), :])
        return jnp.concatenate(parts, axis=0)

    for k in range(4):
        at = slice(LANES * k, LANES * (k + 1))
        gt_ref[at, :main] = r_ref[:, 16 * k : 16 * k + 16].reshape(main, LANES).T
        gt_ref[at, main:] = tails(4 * k).T.astype(jnp.bfloat16)
    at = slice(4 * LANES, TALL)
    last = r_ref[:, 80:88].astype(jnp.float32).reshape(sources * 8, LANES)
    both = jnp.concatenate(
        [last.reshape(sources, 1, 8, LANES), pltpu.roll(last, 96, 1).reshape(sources, 1, 8, LANES)], axis=1
    )
    gt_ref[at, :main] = both.reshape(main, LANES).T[: TALL - 4 * LANES].astype(jnp.bfloat16)
    gt_ref[at, main:] = pltpu.roll(tails(16), 64, 1).T[: TALL - 4 * LANES].astype(jnp.bfloat16)


def time_kernel(r_ref, t_ref, out_ref, gt_ref, tail_ref, held_ref, sem):
    few = out_ref.shape[1]
    step = pl.program_id(0)

    def arrival(n):
        at = pl.ds(pl.multiple_of(n * few, few), few)
        return pltpu.make_async_copy(t_ref.at[at], held_ref.at[at], sem.at[n])

    @pl.when(step == 0)
    def _():
        arrival(0).start()
        arrival(1).start()
        unpack(r_ref, gt_ref, tail_ref)

    @pl.when(step + 2 < pl.num_programs(0))
    def _():
        arrival(step + 2).start()

    arrival(step).wait()
    t = held_ref[pl.ds(pl.multiple_of(step * few, few), few), :]
    w = lax.dot_general(gt_ref[...], t, (((1,), (1,)), ((), ())), preferred_element_type=jnp.float32)
    out_ref[...] = w[:CELLS].astype(jnp.bfloat16)


def time_product(r, t):
    few = 512
    out_rows, total = t.shape
    return pl.pallas_call(
        time_kernel,
        grid=(out_rows // few,),
        in_specs=[WHOLE, OUTSIDE],
        out_specs=pl.BlockSpec((CELLS, few), lambda i: (0, i)),
        out_shape=jax.ShapeDtypeStruct((CELLS, out_rows), jnp.bfloat16),
        scratch_shapes=[
            pltpu.VMEM((TALL, total), jnp.bfloat16),
            pltpu.VMEM((r.shape[0] * (BLOCK - 64), LANES), jnp.float32),
            pltpu.VMEM((out_rows, total), jnp.bfloat16),
            pltpu.SemaphoreType.DMA((out_rows // few,)),
        ],
        compiler_params=params(40),
    )(r, t)


def by_thirds(lat_factor):
    rows = lat_factor.shape[0]
    return lat_factor.reshape(rows // 3, 3, rows).transpose(1, 0, 2).reshape(rows, rows)


def on_device(field, time_factor, lat_factor, lon_factor):
    hours, few, columns = field.shape
    parts = lax.axis_size("lat")
    moved = lax.all_to_all(field, "lat", split_axis=0, concat_axis=0, tiled=True)
    ordered = order_columns(time_factor)
    lat = by_thirds(lat_factor)
    blocks = mix(moved.reshape(parts, hours // parts, few, columns), lon_factor, lat)
    got = lax.all_to_all(blocks, ("tm", "lat"), split_axis=0, concat_axis=0, tiled=True)
    return time_product(got, ordered).T


def solution(mesh):
    return jax.shard_map(
        on_device,
        mesh=mesh,
        in_specs=(P("tm", "lat", None), P(), P(), P()),
        out_specs=P(None, ("tm", "lat")),
        check_vma=False,
    )
```

time: 148 us -> 111 us (0.75)
  blocking collectives: 100 us -> 0 us
  waiting for transfers between devices: 0 us -> 49.6 us
  Pallas kernels: 0 us -> 31.9 us
  matrix products: 20.6 us -> 0 us
  starting transfers between devices: 0 us -> 16.7 us
  local copies, waits for them, and re-layouts: 25 us -> 11 us
    all_to_all x2 -> x0, blocking collectives: 100 us -> none  [the longest x1 56.6 us: on_device(): lax.all_to_all(second, ('tm', 'lat'), split_axis=1, concat_axis=0, tiled=...]
    all_to_all x0 -> x2, waiting for transfers between devices: none -> 49.6 us  [the longest x1 35.2 us: on_device(): lax.all_to_all(field, 'lat', split_axis=0, concat_axis=0, tiled=True)]
    pallas_call x0 -> x3, Pallas kernels: none -> 31.9 us  [the longest x1 13.3 us: order_columns(): pl.pallas_call(order_kernel, grid=(rows // few,), in_specs=[pl.BlockSpec(...]
    dot_general x3 -> x0, matrix products: 20.6 us -> none  [the longest x1 14 us: on_device(): weights = jnp.dot(time_factor, gathered, preferred_element_type=jnp.float32)]
    all_to_all x4 -> x0, local copies, waits for them, and re-layouts: 18.4 us -> none  [the longest x3 17.9 us: on_device(): lax.all_to_all(second, ('tm', 'lat'), split_axis=1, concat_axis=0, tiled=...]
    all_to_all x0 -> x2, starting transfers between devices: none -> 16.7 us  [the longest x1 9.04 us: on_device(): lax.all_to_all(blocks, ('tm', 'lat'), split_axis=0, concat_axis=0, tiled=...]
    unnamed x4 -> x10, local copies, waits for them, and re-layouts: 2.2 us -> 10.9 us
    convert_element_type x1 -> x0, local copies, waits for them, and re-layouts: 4.46 us -> none  [on_device(): first = first.astype(jnp.bfloat16).reshape(hours, rows, columns)]
  transfers between devices with their start and end apart: 0 -> 2, of which waited for: 0 -> 2; matrix products, arithmetic and copies ran while one was open for 0% -> 0% of each run, Pallas kernels for 0% -> 12%
where the time goes in v2:
time: 111 us; the launch traced here: 110 us
  waiting for transfers between devices  49.6 us (45%)
  Pallas kernels  31.9 us (29%)
  starting transfers between devices  16.7 us (15%)
  local copies, waits for them, and re-layouts  11 us (10%)
    all_to_all x1, waiting for transfers between devices, on_device(): lax.all_to_all(field, 'lat', split_axis=0, concat_axis=0, tiled=True)  35.2 us
    all_to_all x1, waiting for transfers between devices, on_device(): lax.all_to_all(blocks, ('tm', 'lat'), split_axis=0, concat_axis=0, tiled=...  14.4 us
    pallas_call x1, Pallas kernels, order_columns(): pl.pallas_call(order_kernel, grid=(rows // few,), in_specs=[pl.BlockSpec(...  13.3 us
    unnamed x10, local copies, waits for them, and re-layouts  10.9 us
    pallas_call x1, Pallas kernels, time_product(): pl.pallas_call(time_kernel, grid=(out_rows // few,), in_specs=[WHOLE, OUT...  10.8 us
    all_to_all x1, starting transfers between devices, on_device(): lax.all_to_all(blocks, ('tm', 'lat'), split_axis=0, concat_axis=0, tiled=...  9.04 us
    pallas_call x1, Pallas kernels, mix(): pl.pallas_call(mix_kernel, in_specs=[WHOLE] * 3, out_specs=OUTSIDE, out_s...  7.78 us
    all_to_all x1, starting transfers between devices, on_device(): lax.all_to_all(field, 'lat', split_axis=0, concat_axis=0, tiled=True)  7.61 us
  transfers between devices with their start and end apart: 2, of which 2 were waited for; matrix products, arithmetic and copies ran while one was open for 0% of the time, Pallas kernels for 12%

profile of v2, /device:TPU:1, one launch (start us, length us, event | category | flops | bytes accessed | tf_op | source)
XLA Modules:
  0.0 109.5 jit_solution(8763556124518820012)
XLA Ops:
  0.0 0.0 copy-start.4
  0.0 0.0 copy-start.3
  0.0 7.6 %all-to-all-start = ((bf16[160,24,360]{2,1,0:T(8,128)(2,1)}), bf16[160,24,360]{2,1,0:T(8,128)(2,1)S(1)}, u32[]{:S(2)}, u32[]{:S(2)}) async-start(bf16[160,24,360]{2,1,0:T(8,128)(2,1)} %param.4), calls=%async_computation | async-start | bytes 5898240 | tf_op jit(solution)/shard_map/all_to_all | solution.py:237
  7.6 0.0 copy-done.4
  7.6 0.1 reshape.66
  7.7 35.2 %all-to-all-done = bf16[160,24,360]{2,1,0:T(8,128)(2,1)S(1)} async-done(((bf16[160,24,360]{2,1,0:T(8,128)(2,1)}), bf16[160,24,360]{2,1,0:T(8,128)(2,1)S(1)}, u32[]{:S(2)}, u32[]{:S(2)}) %all-to-all-start) | async-done | bytes 2764832 | tf_op jit(solution)/shard_map/all_to_all | solution.py:237
  42.9 0.0 copy-done.3
  42.9 7.8 %shard_map.46 = bf16[128,88,128]{2,1,0:T(8,128)(2,1)S(1)} custom-call(bf16[8,20,24,360]{3,2,1,0:T(8,128)(2,1)S(1)} %bitcast.4, bf16[360,360]{1,0:T(8,128)(2,1)S(1)} %copy-done.3, bf16[192,192]{1,0:T(8,128)(2,1)S(1)} %bitcast.5), custom_call_target="tpu_custom_call" | custom-call | tf_op jit(solution)/shard_map/pallas_call | solution.py:116
  50.7 0.0 copy-start.2
  50.7 1.5 %copy-done.2 = bf16[128,88,128]{2,1,0:T(8,128)(2,1)} copy-done((bf16[128,88,128]{2,1,0:T(8,128)(2,1)}, bf16[128,88,128]{2,1,0:T(8,128)(2,1)S(1)}, u32[]{:S(2)}) %copy-start.2) | copy-done | bytes 2883608
  52.2 9.0 %all-to-all-start.1 = ((bf16[128,88,128]{2,1,0:T(8,128)(2,1)}), bf16[128,88,128]{2,1,0:T(8,128)(2,1)S(1)}, u32[]{:S(2)}, u32[]{:S(2)}) async-start(bf16[128,88,128]{2,1,0:T(8,128)(2,1)} %copy-done.2), calls=%async_computation.1 | async-start | bytes 5767168 | tf_op jit(solution)/shard_map/all_to_all | solution.py:241
  61.3 0.2 fusion.move_ref
  61.6 0.0 copy-start.1
  61.6 4.7 %copy-done.1 = bf16[2560,2560]{1,0:T(8,128)(2,1)S(1)} copy-done((bf16[2560,2560]{1,0:T(8,128)(2,1)S(1)}, bf16[2560,2560]{1,0:T(8,128)(2,1)}, u32[]{:S(2)}) %copy-start.1) | copy-done | bytes 13107224
  66.3 13.3 %shard_map.47.t_ref = bf16[2560,2560]{1,0:T(8,128)(2,1)S(1)} custom-call(bf16[2560,2560]{1,0:T(8,128)(2,1)S(1)} %copy-done.1, bf16[640,640]{1,0:T(8,128)(2,1)S(1)} %fusion.move_ref), custom_call_target="tpu_custom_call" | custom-call | tf_op jit(solution)/shard_map/pallas_call | solution.py:150
  79.6 0.0 copy-start
  79.6 4.7 %copy-done = bf16[2560,2560]{1,0:T(8,128)(2,1)} copy-done((bf16[2560,2560]{1,0:T(8,128)(2,1)}, bf16[2560,2560]{1,0:T(8,128)(2,1)S(1)}, u32[]{:S(2)}) %copy-start) | copy-done | bytes 13107224
  84.3 14.4 %all-to-all-done.1.r_ref = bf16[128,88,128]{2,1,0:T(8,128)(2,1)S(1)} async-done(((bf16[128,88,128]{2,1,0:T(8,128)(2,1)}), bf16[128,88,128]{2,1,0:T(8,128)(2,1)S(1)}, u32[]{:S(2)}, u32[]{:S(2)}) %all-to-all-start.1) | async-done | bytes 2883616 | tf_op jit(solution)/shard_map/all_to_all | solution.py:241
  98.7 10.8 %shard_map.48 = bf16[540,2560]{1,0:T(8,128)(2,1)} custom-call(bf16[128,88,128]{2,1,0:T(8,128)(2,1)S(1)} %all-to-all-done.1.r_ref, bf16[2560,2560]{1,0:T(8,128)(2,1)} %copy-done), custom_call_target="tpu_custom_call" | custom-call | tf_op jit(solution)/shard_map/pallas_call | solution.py:213
  (2 shorter events, 0.0 us)
Async XLA Ops:
  0.0 7.6 %copy-start.4 = (bf16[192,192]{1,0:T(8,128)(2,1)S(1)}, bf16[192,192]{1,0:T(8,128)(2,1)}, u32[]{:S(2)}) copy-start(bf16[192,192]{1,0:T(8,128)(2,1)} %param.6) | copy-start | bytes 221188
  0.0 42.9 %copy-start.3 = (bf16[360,360]{1,0:T(8,128)(2,1)S(1)}, bf16[360,360]{1,0:T(8,128)(2,1)}, u32[]{:S(2)}) copy-start(bf16[360,360]{1,0:T(8,128)(2,1)} %lon_ref.1) | copy-start | bytes 777604
  0.0 42.9 %all-to-all-start = ((bf16[160,24,360]{2,1,0:T(8,128)(2,1)}), bf16[160,24,360]{2,1,0:T(8,128)(2,1)S(1)}, u32[]{:S(2)}, u32[]{:S(2)}) async-start(bf16[160,24,360]{2,1,0:T(8,128)(2,1)} %param.4), calls=%async_computation | async-start | bytes 5898240 | tf_op jit(solution)/shard_map/all_to_all | solution.py:237
  50.7 1.6 %copy-start.2 = (bf16[128,88,128]{2,1,0:T(8,128)(2,1)}, bf16[128,88,128]{2,1,0:T(8,128)(2,1)S(1)}, u32[]{:S(2)}) copy-start(bf16[128,88,128]{2,1,0:T(8,128)(2,1)S(1)} %shard_map.46) | copy-start | bytes 8650756
  52.2 46.5 %all-to-all-start.1 = ((bf16[128,88,128]{2,1,0:T(8,128)(2,1)}), bf16[128,88,128]{2,1,0:T(8,128)(2,1)S(1)}, u32[]{:S(2)}, u32[]{:S(2)}) async-start(bf16[128,88,128]{2,1,0:T(8,128)(2,1)} %copy-done.2), calls=%async_computation.1 | async-start | bytes 5767168 | tf_op jit(solution)/shard_map/all_to_all | solution.py:241
  61.6 4.7 %copy-start.1 = (bf16[2560,2560]{1,0:T(8,128)(2,1)S(1)}, bf16[2560,2560]{1,0:T(8,128)(2,1)}, u32[]{:S(2)}) copy-start(bf16[2560,2560]{1,0:T(8,128)(2,1)} %t_ref.1) | copy-start | bytes 39321604
  79.6 4.7 %copy-start = (bf16[2560,2560]{1,0:T(8,128)(2,1)}, bf16[2560,2560]{1,0:T(8,128)(2,1)S(1)}, u32[]{:S(2)}) copy-start(bf16[2560,2560]{1,0:T(8,128)(2,1)S(1)} %shard_map.47.t_ref) | copy-start | bytes 39321604

commit v3 on v2

--- a/solution.py
+++ b/solution.py
@@ -117,7 +117,7 @@
         mix_kernel,
         in_specs=[WHOLE] * 3,
         out_specs=OUTSIDE,
-        out_shape=jax.ShapeDtypeStruct((2 * rows // 3, BLOCK, LANES), jnp.bfloat16),
+        out_shape=pltpu.HBM((2 * rows // 3, BLOCK, LANES), jnp.bfloat16),
         scratch_shapes=[
             pltpu.VMEM((parts, hours, few, columns), jnp.float32),
             pltpu.VMEM((3, 24 * STRIDE, LANES), jnp.float32),

time: 111 us -> 109 us (0.982)
  local copies, waits for them, and re-layouts: 11 us -> 9.46 us
    unnamed x10 -> x8, local copies, waits for them, and re-layouts: 10.9 us -> 9.39 us
where the time goes in v3:
time: 109 us; the launch traced here: 108 us
  waiting for transfers between devices  49.6 us (46%)
  Pallas kernels  31.5 us (29%)
  starting transfers between devices  16.7 us (15%)
  local copies, waits for them, and re-layouts  9.46 us (9%)
    all_to_all x1, waiting for transfers between devices, on_device(): lax.all_to_all(field, 'lat', split_axis=0, concat_axis=0, tiled=True)  35.2 us
    all_to_all x1, waiting for transfers between devices, on_device(): lax.all_to_all(blocks, ('tm', 'lat'), split_axis=0, concat_axis=0, tiled=...  14.4 us
    pallas_call x1, Pallas kernels, order_columns(): pl.pallas_call(order_kernel, grid=(rows // few,), in_specs=[pl.BlockSpec(...  13.3 us
    pallas_call x1, Pallas kernels, time_product(): pl.pallas_call(time_kernel, grid=(out_rows // few,), in_specs=[WHOLE, OUT...  10.8 us
    unnamed x8, local copies, waits for them, and re-layouts  9.39 us
    all_to_all x1, starting transfers between devices, on_device(): lax.all_to_all(blocks, ('tm', 'lat'), split_axis=0, concat_axis=0, tiled=...  9.05 us
    all_to_all x1, starting transfers between devices, on_device(): lax.all_to_all(field, 'lat', split_axis=0, concat_axis=0, tiled=True)  7.61 us
    pallas_call x1, Pallas kernels, mix(): pl.pallas_call(mix_kernel, in_specs=[WHOLE] * 3, out_specs=OUTSIDE, out_s...  7.34 us
  transfers between devices with their start and end apart: 2, of which 2 were waited for; matrix products, arithmetic and copies ran while one was open for 0% of the time, Pallas kernels for 12%

profile of v3, /device:TPU:1, one launch (start us, length us, event | category | flops | bytes accessed | tf_op | source)
XLA Modules:
  0.0 107.5 jit_solution(2095454647395007802)
XLA Ops:
  0.0 0.0 copy-start.3
  0.0 0.0 copy-start.2
  0.0 7.6 %all-to-all-start = ((bf16[160,24,360]{2,1,0:T(8,128)(2,1)}), bf16[160,24,360]{2,1,0:T(8,128)(2,1)S(1)}, u32[]{:S(2)}, u32[]{:S(2)}) async-start(bf16[160,24,360]{2,1,0:T(8,128)(2,1)} %param.4), calls=%async_computation | async-start | bytes 5898240 | tf_op jit(solution)/shard_map/all_to_all | solution.py:237
  7.6 0.0 copy-done.3
  7.6 0.1 reshape.66
  7.7 35.2 %all-to-all-done = bf16[160,24,360]{2,1,0:T(8,128)(2,1)S(1)} async-done(((bf16[160,24,360]{2,1,0:T(8,128)(2,1)}), bf16[160,24,360]{2,1,0:T(8,128)(2,1)S(1)}, u32[]{:S(2)}, u32[]{:S(2)}) %all-to-all-start) | async-done | bytes 2764832 | tf_op jit(solution)/shard_map/all_to_all | solution.py:237
  42.9 0.0 copy-done.2
  42.9 7.3 %shard_map.46 = bf16[128,88,128]{2,1,0:T(8,128)(2,1)} custom-call(bf16[8,20,24,360]{3,2,1,0:T(8,128)(2,1)S(1)} %bitcast.4, bf16[360,360]{1,0:T(8,128)(2,1)S(1)} %copy-done.2, bf16[192,192]{1,0:T(8,128)(2,1)S(1)} %bitcast.5), custom_call_target="tpu_custom_call" | custom-call | tf_op jit(solution)/shard_map/pallas_call | solution.py:116
  50.2 9.0 %all-to-all-start.1 = ((bf16[128,88,128]{2,1,0:T(8,128)(2,1)}), bf16[128,88,128]{2,1,0:T(8,128)(2,1)S(1)}, u32[]{:S(2)}, u32[]{:S(2)}) async-start(bf16[128,88,128]{2,1,0:T(8,128)(2,1)} %shard_map.46), calls=%async_computation.1 | async-start | bytes 5767168 | tf_op jit(solution)/shard_map/all_to_all | solution.py:241
  59.3 0.2 fusion.move_ref
  59.6 0.0 copy-start.1
  59.6 4.7 %copy-done.1 = bf16[2560,2560]{1,0:T(8,128)(2,1)S(1)} copy-done((bf16[2560,2560]{1,0:T(8,128)(2,1)S(1)}, bf16[2560,2560]{1,0:T(8,128)(2,1)}, u32[]{:S(2)}) %copy-start.1) | copy-done | bytes 13107224
  64.3 13.3 %shard_map.47.t_ref = bf16[2560,2560]{1,0:T(8,128)(2,1)S(1)} custom-call(bf16[2560,2560]{1,0:T(8,128)(2,1)S(1)} %copy-done.1, bf16[640,640]{1,0:T(8,128)(2,1)S(1)} %fusion.move_ref), custom_call_target="tpu_custom_call" | custom-call | tf_op jit(solution)/shard_map/pallas_call | solution.py:150
  77.6 0.0 copy-start
  77.6 4.7 %copy-done = bf16[2560,2560]{1,0:T(8,128)(2,1)} copy-done((bf16[2560,2560]{1,0:T(8,128)(2,1)}, bf16[2560,2560]{1,0:T(8,128)(2,1)S(1)}, u32[]{:S(2)}) %copy-start) | copy-done | bytes 13107224
  82.3 14.4 %all-to-all-done.1.r_ref = bf16[128,88,128]{2,1,0:T(8,128)(2,1)S(1)} async-done(((bf16[128,88,128]{2,1,0:T(8,128)(2,1)}), bf16[128,88,128]{2,1,0:T(8,128)(2,1)S(1)}, u32[]{:S(2)}, u32[]{:S(2)}) %all-to-all-start.1) | async-done | bytes 2883616 | tf_op jit(solution)/shard_map/all_to_all | solution.py:241
  96.7 10.8 %shard_map.48 = bf16[540,2560]{1,0:T(8,128)(2,1)} custom-call(bf16[128,88,128]{2,1,0:T(8,128)(2,1)S(1)} %all-to-all-done.1.r_ref, bf16[2560,2560]{1,0:T(8,128)(2,1)} %copy-done), custom_call_target="tpu_custom_call" | custom-call | tf_op jit(solution)/shard_map/pallas_call | solution.py:213
  (2 shorter events, 0.0 us)
Async XLA Ops:
  0.0 7.6 %copy-start.3 = (bf16[192,192]{1,0:T(8,128)(2,1)S(1)}, bf16[192,192]{1,0:T(8,128)(2,1)}, u32[]{:S(2)}) copy-start(bf16[192,192]{1,0:T(8,128)(2,1)} %param.6) | copy-start | bytes 221188
  0.0 42.9 %copy-start.2 = (bf16[360,360]{1,0:T(8,128)(2,1)S(1)}, bf16[360,360]{1,0:T(8,128)(2,1)}, u32[]{:S(2)}) copy-start(bf16[360,360]{1,0:T(8,128)(2,1)} %lon_ref.1) | copy-start | bytes 777604
  0.0 42.9 %all-to-all-start = ((bf16[160,24,360]{2,1,0:T(8,128)(2,1)}), bf16[160,24,360]{2,1,0:T(8,128)(2,1)S(1)}, u32[]{:S(2)}, u32[]{:S(2)}) async-start(bf16[160,24,360]{2,1,0:T(8,128)(2,1)} %param.4), calls=%async_computation | async-start | bytes 5898240 | tf_op jit(solution)/shard_map/all_to_all | solution.py:237
  50.2 46.5 %all-to-all-start.1 = ((bf16[128,88,128]{2,1,0:T(8,128)(2,1)}), bf16[128,88,128]{2,1,0:T(8,128)(2,1)S(1)}, u32[]{:S(2)}, u32[]{:S(2)}) async-start(bf16[128,88,128]{2,1,0:T(8,128)(2,1)} %shard_map.46), calls=%async_computation.1 | async-start | bytes 5767168 | tf_op jit(solution)/shard_map/all_to_all | solution.py:241
  59.6 4.7 %copy-start.1 = (bf16[2560,2560]{1,0:T(8,128)(2,1)S(1)}, bf16[2560,2560]{1,0:T(8,128)(2,1)}, u32[]{:S(2)}) copy-start(bf16[2560,2560]{1,0:T(8,128)(2,1)} %t_ref.1) | copy-start | bytes 39321604
  77.6 4.7 %copy-start = (bf16[2560,2560]{1,0:T(8,128)(2,1)}, bf16[2560,2560]{1,0:T(8,128)(2,1)S(1)}, u32[]{:S(2)}) copy-start(bf16[2560,2560]{1,0:T(8,128)(2,1)S(1)} %shard_map.47.t_ref) | copy-start | bytes 39321604

commit v4 on v3

--- a/solution.py
+++ b/solution.py
@@ -66,7 +66,7 @@
     lane8 = lax.broadcasted_iota(jnp.int32, (8, LANES), 1)
     lane = lax.broadcasted_iota(jnp.int32, (24, LANES), 1)
 
-    def triple(p, carry):
+    def triple(p, even, odd):
         a, b, c = (
             jnp.concatenate(
                 [second_ref[jnp.int32(k), pl.ds(jnp.int32(r * third) + p, 24, STRIDE), :] for k in range(3)], axis=1
@@ -74,14 +74,14 @@
             for r in range(3)
         )
         b_up = pltpu.roll(b, 104, 1)
-        out_ref[2 * p] = pack(
+        out_ref[even] = pack(
             [tile(a, 0), tile(a, 1), jnp.where(lane < 104, tile(a, 2), tile(b_up, 0)), tile(b_up, 1), tile(b_up, 2)],
             row,
             lane8,
         )
         b_down = pltpu.roll(b, 204, 1)
         c_up = pltpu.roll(c, 180, 1)
-        out_ref[2 * p + 1] = pack(
+        out_ref[odd] = pack(
             [
                 tile(b_down, 0),
                 jnp.where(lane < 52, tile(b_down, 1), tile(c_up, 1)),
@@ -92,7 +92,6 @@
             row,
             lane8,
         )
-        return carry
 
     each = out_ref.shape[0] // COPIES
 
@@ -101,7 +100,16 @@
         return pltpu.make_async_copy(out_ref.at[at], to_ref.at[at], sem.at[n])
 
     def some(n, carry):
-        lax.fori_loop(0, each // 8, lambda q, c: [triple(n * (each // 2) + 4 * q + i, c) for i in range(4)][-1], 0)
+        core, z = n // 4, n % 4
+
+        def four(x_lo, inner):
+            for i in range(4):
+                x_hi, y = i // 2, i % 2 * 2
+                at = n * each + y * 4 + x_hi * 2 + x_lo
+                triple(z * 16 + x_lo * 8 + core * 4 + i, at, at + 4)
+            return inner
+
+        lax.fori_loop(0, 2, four, 0)
         leave(n).start()
         return carry
 
@@ -131,20 +139,35 @@
 def order_kernel(t_ref, move_ref, out_ref):
     move = move_ref[...]
     total = t_ref.shape[1]
-    main = 32 * MAIN
-    tail = GROUP - main
-    for u in range(total // GROUP):
-        w = jnp.dot(t_ref[:, GROUP * u : GROUP * (u + 1)], move, preferred_element_type=jnp.float32).astype(jnp.bfloat16)
-        out_ref[:, main * u : main * (u + 1)] = w[:, :main]
-        start = total // GROUP * main + tail * u
-        out_ref[:, start : start + tail] = w[:, main:]
+    groups = total // GROUP
+    main, tail = 16 * MAIN, 16 * (HOURS - MAIN)
+    tails = []
+    for z in range(groups):
+        w = jnp.dot(t_ref[:, GROUP * z : GROUP * (z + 1)], move, preferred_element_type=jnp.float32)
+        for core in range(2):
+            at = (core * groups + z) * main
+            out_ref[:, at : at + main] = w[:, main * core : main * (core + 1)].astype(jnp.bfloat16)
+        tails.append(w[:, 2 * main :])
+    low = lax.broadcasted_iota(jnp.int32, tails[0].shape, 1) < tail
+    start = 2 * groups * main
+    for z in range(0, groups, 2):
+        x, y = tails[z], tails[z + 1]
+        for core, both in enumerate((jnp.where(low, x, pltpu.roll(y, tail, 1)), jnp.where(low, pltpu.roll(x, tail, 1), y))):
+            at = start + (core * groups + z) * tail
+            out_ref[:, at : at + 2 * tail] = both.astype(jnp.bfloat16)
 
 
 def order_columns(time_factor):
     rows, total = time_factor.shape
     col = jnp.arange(GROUP)
-    main = 32 * MAIN
-    hour = jnp.where(col < main, col // MAIN * HOURS + col % MAIN, (col - main) % 32 * HOURS + MAIN + (col - main) // 32)
+    main, tail = 16 * MAIN, 16 * (HOURS - MAIN)
+    late = col >= 2 * main
+    core = jnp.where(late, (col - 2 * main) // tail, col // main)
+    within = jnp.where(late, (col - 2 * main) % tail, col % main)
+    device = jnp.where(late, within % 16, within // MAIN)
+    which = jnp.where(late, MAIN + within // 16, within % MAIN)
+    y, x_hi, x_lo = device // 4, device // 2 % 2, device % 2
+    hour = (x_lo * 2 + core) * 8 * HOURS + (x_hi * 4 + y) * HOURS + which
     move = (jnp.arange(GROUP)[:, None] == hour[None, :]).astype(jnp.bfloat16)
     few = 256
     return pl.pallas_call(
@@ -165,9 +188,9 @@
 
     def tails(first):
         parts = []
-        for u in range(sources // 32):
+        for u in range(sources // 16):
             for i in range(HOURS - MAIN):
-                parts.append(tail_ref[pl.ds(u * 32 * few + first + i, 32, few), :])
+                parts.append(tail_ref[pl.ds(u * 16 * few + first + i, 16, few), :])
         return jnp.concatenate(parts, axis=0)
 
     for k in range(4):
@@ -233,20 +256,22 @@
 
 def on_device(field, time_factor, lat_factor, lon_factor):
     hours, few, columns = field.shape
-    parts = lax.axis_size("lat")
-    moved = lax.all_to_all(field, "lat", split_axis=0, concat_axis=0, tiled=True)
+    parts = lax.axis_size(("x_hi", "y"))
+    moved = lax.all_to_all(field, ("x_hi", "y"), split_axis=0, concat_axis=0, tiled=True)
     ordered = order_columns(time_factor)
     lat = by_thirds(lat_factor)
     blocks = mix(moved.reshape(parts, hours // parts, few, columns), lon_factor, lat)
-    got = lax.all_to_all(blocks, ("tm", "lat"), split_axis=0, concat_axis=0, tiled=True)
+    got = lax.all_to_all(blocks, ("core", "z", "y", "x_hi", "x_lo"), split_axis=0, concat_axis=0, tiled=True)
     return time_product(got, ordered).T
 
 
 def solution(mesh):
+    tm, lat = ("z", "x_lo", "core"), ("x_hi", "y")
+    parts = jax.sharding.Mesh(mesh.devices.reshape(4, 2, 2, 2, 4), tm + lat)
     return jax.shard_map(
         on_device,
-        mesh=mesh,
-        in_specs=(P("tm", "lat", None), P(), P(), P()),
-        out_specs=P(None, ("tm", "lat")),
+        mesh=parts,
+        in_specs=(P(tm, lat, None), P(), P(), P()),
+        out_specs=P(None, tm + lat),
         check_vma=False,
     )

time: 109 us -> 108 us (level)
  waiting for transfers between devices: 49.6 us -> 48.5 us
    all_to_all x2, waiting for transfers between devices: 49.6 us -> 48.5 us  [the longest x1 35.2 us: on_device(): lax.all_to_all(field, ('x_hi', 'y'), split_axis=0, concat_axis=0, tiled=T...]
  transfers between devices with their start and end apart: 2 -> 2, of which waited for: 2 -> 2; matrix products, arithmetic and copies ran while one was open for 0% -> 0% of each run, Pallas kernels for 12% -> 13%
where the time goes in v4:
time: 108 us; the launch traced here: 107 us
  waiting for transfers between devices  48.5 us (45%)
  Pallas kernels  32.2 us (30%)
  starting transfers between devices  16.7 us (15%)
  local copies, waits for them, and re-layouts  9.46 us (9%)
    all_to_all x1, waiting for transfers between devices, on_device(): lax.all_to_all(field, ('x_hi', 'y'), split_axis=0, concat_axis=0, tiled=T...  35.2 us
    pallas_call x1, Pallas kernels, order_columns(): pl.pallas_call(order_kernel, grid=(rows // few,), in_specs=[pl.BlockSpec(...  14 us
    all_to_all x1, waiting for transfers between devices, on_device(): lax.all_to_all(blocks, ('core', 'z', 'y', 'x_hi', 'x_lo'), split_axis=0,...  13.3 us
    pallas_call x1, Pallas kernels, time_product(): pl.pallas_call(time_kernel, grid=(out_rows // few,), in_specs=[WHOLE, OUT...  10.8 us
    unnamed x8, local copies, waits for them, and re-layouts  9.39 us
    all_to_all x1, starting transfers between devices, on_device(): lax.all_to_all(blocks, ('core', 'z', 'y', 'x_hi', 'x_lo'), split_axis=0,...  9.05 us
    all_to_all x1, starting transfers between devices, on_device(): lax.all_to_all(field, ('x_hi', 'y'), split_axis=0, concat_axis=0, tiled=T...  7.61 us
    pallas_call x1, Pallas kernels, mix(): pl.pallas_call(mix_kernel, in_specs=[WHOLE] * 3, out_specs=OUTSIDE, out_s...  7.37 us
  transfers between devices with their start and end apart: 2, of which 2 were waited for; matrix products, arithmetic and copies ran while one was open for 0% of the time, Pallas kernels for 13%

profile of v4, /device:TPU:1, one launch (start us, length us, event | category | flops | bytes accessed | tf_op | source)
XLA Modules:
  0.0 107.2 jit_solution(15189969032521261058)
XLA Ops:
  0.0 0.0 copy-start.3
  0.0 0.0 copy-start.2
  0.0 7.6 %all-to-all-start = ((bf16[160,24,360]{2,1,0:T(8,128)(2,1)}), bf16[160,24,360]{2,1,0:T(8,128)(2,1)S(1)}, u32[]{:S(2)}, u32[]{:S(2)}) async-start(bf16[160,24,360]{2,1,0:T(8,128)(2,1)} %param.4), calls=%async_computation | async-start | bytes 5898240 | tf_op jit(solution)/shard_map/all_to_all | solution.py:260
  7.6 0.0 copy-done.3
  7.6 0.1 reshape.146
  7.7 35.2 %all-to-all-done = bf16[160,24,360]{2,1,0:T(8,128)(2,1)S(1)} async-done(((bf16[160,24,360]{2,1,0:T(8,128)(2,1)}), bf16[160,24,360]{2,1,0:T(8,128)(2,1)S(1)}, u32[]{:S(2)}, u32[]{:S(2)}) %all-to-all-start) | async-done | bytes 2764832 | tf_op jit(solution)/shard_map/all_to_all | solution.py:260
  42.9 0.0 copy-done.2
  42.9 7.4 %shard_map.46 = bf16[128,88,128]{2,1,0:T(8,128)(2,1)} custom-call(bf16[8,20,24,360]{3,2,1,0:T(8,128)(2,1)S(1)} %bitcast.4, bf16[360,360]{1,0:T(8,128)(2,1)S(1)} %copy-done.2, bf16[192,192]{1,0:T(8,128)(2,1)S(1)} %bitcast.5), custom_call_target="tpu_custom_call" | custom-call | tf_op jit(solution)/shard_map/pallas_call | solution.py:124
  50.3 9.0 %all-to-all-start.1 = ((bf16[128,88,128]{2,1,0:T(8,128)(2,1)}), bf16[128,88,128]{2,1,0:T(8,128)(2,1)S(1)}, u32[]{:S(2)}, u32[]{:S(2)}) async-start(bf16[128,88,128]{2,1,0:T(8,128)(2,1)} %shard_map.46), calls=%async_computation.1 | async-start | bytes 5767168 | tf_op jit(solution)/shard_map/all_to_all | solution.py:264
  59.4 0.3 fusion.move_ref
  59.6 0.0 copy-start.1
  59.6 4.7 %copy-done.1 = bf16[2560,2560]{1,0:T(8,128)(2,1)S(1)} copy-done((bf16[2560,2560]{1,0:T(8,128)(2,1)S(1)}, bf16[2560,2560]{1,0:T(8,128)(2,1)}, u32[]{:S(2)}) %copy-start.1) | copy-done | bytes 13107224
  64.3 14.0 %shard_map.47.t_ref = bf16[2560,2560]{1,0:T(8,128)(2,1)S(1)} custom-call(bf16[2560,2560]{1,0:T(8,128)(2,1)S(1)} %copy-done.1, bf16[640,640]{1,0:T(8,128)(2,1)S(1)} %fusion.move_ref), custom_call_target="tpu_custom_call" | custom-call | tf_op jit(solution)/shard_map/pallas_call | solution.py:173
  78.4 0.0 copy-start
  78.4 4.7 %copy-done = bf16[2560,2560]{1,0:T(8,128)(2,1)} copy-done((bf16[2560,2560]{1,0:T(8,128)(2,1)}, bf16[2560,2560]{1,0:T(8,128)(2,1)S(1)}, u32[]{:S(2)}) %copy-start) | copy-done | bytes 13107224
  83.1 13.3 %all-to-all-done.1.r_ref = bf16[128,88,128]{2,1,0:T(8,128)(2,1)S(1)} async-done(((bf16[128,88,128]{2,1,0:T(8,128)(2,1)}), bf16[128,88,128]{2,1,0:T(8,128)(2,1)S(1)}, u32[]{:S(2)}, u32[]{:S(2)}) %all-to-all-start.1) | async-done | bytes 2883616 | tf_op jit(solution)/shard_map/all_to_all | solution.py:264
  96.4 10.8 %shard_map.48 = bf16[540,2560]{1,0:T(8,128)(2,1)} custom-call(bf16[128,88,128]{2,1,0:T(8,128)(2,1)S(1)} %all-to-all-done.1.r_ref, bf16[2560,2560]{1,0:T(8,128)(2,1)} %copy-done), custom_call_target="tpu_custom_call" | custom-call | tf_op jit(solution)/shard_map/pallas_call | solution.py:236
  (2 shorter events, 0.1 us)
Async XLA Ops:
  0.0 7.6 %copy-start.3 = (bf16[192,192]{1,0:T(8,128)(2,1)S(1)}, bf16[192,192]{1,0:T(8,128)(2,1)}, u32[]{:S(2)}) copy-start(bf16[192,192]{1,0:T(8,128)(2,1)} %param.6) | copy-start | bytes 221188
  0.0 42.9 %copy-start.2 = (bf16[360,360]{1,0:T(8,128)(2,1)S(1)}, bf16[360,360]{1,0:T(8,128)(2,1)}, u32[]{:S(2)}) copy-start(bf16[360,360]{1,0:T(8,128)(2,1)} %lon_ref.1) | copy-start | bytes 777604
  0.0 42.9 %all-to-all-start = ((bf16[160,24,360]{2,1,0:T(8,128)(2,1)}), bf16[160,24,360]{2,1,0:T(8,128)(2,1)S(1)}, u32[]{:S(2)}, u32[]{:S(2)}) async-start(bf16[160,24,360]{2,1,0:T(8,128)(2,1)} %param.4), calls=%async_computation | async-start | bytes 5898240 | tf_op jit(solution)/shard_map/all_to_all | solution.py:260
  50.3 46.1 %all-to-all-start.1 = ((bf16[128,88,128]{2,1,0:T(8,128)(2,1)}), bf16[128,88,128]{2,1,0:T(8,128)(2,1)S(1)}, u32[]{:S(2)}, u32[]{:S(2)}) async-start(bf16[128,88,128]{2,1,0:T(8,128)(2,1)} %shard_map.46), calls=%async_computation.1 | async-start | bytes 5767168 | tf_op jit(solution)/shard_map/all_to_all | solution.py:264
  59.6 4.7 %copy-start.1 = (bf16[2560,2560]{1,0:T(8,128)(2,1)S(1)}, bf16[2560,2560]{1,0:T(8,128)(2,1)}, u32[]{:S(2)}) copy-start(bf16[2560,2560]{1,0:T(8,128)(2,1)} %t_ref.1) | copy-start | bytes 39321604
  78.4 4.7 %copy-start = (bf16[2560,2560]{1,0:T(8,128)(2,1)}, bf16[2560,2560]{1,0:T(8,128)(2,1)S(1)}, u32[]{:S(2)}) copy-start(bf16[2560,2560]{1,0:T(8,128)(2,1)S(1)} %shard_map.47.t_ref) | copy-start | bytes 39321604

commit v5 on v4

--- a/solution.py
+++ b/solution.py
@@ -49,7 +49,7 @@
         first_ref[part] = first.reshape(hours, few, columns)
         return carry
 
-    lax.fori_loop(0, parts, part_of_first, 0, unroll=4)
+    lax.fori_loop(0, parts, part_of_first, 0, unroll=8)
     lat = lat_ref[...]
 
     def hour(t, carry):
@@ -61,7 +61,7 @@
             second_ref[k, at, :width] = s[:, LANES * k : LANES * k + width]
         return carry
 
-    lax.fori_loop(0, hours, hour, 0, unroll=10)
+    lax.fori_loop(0, hours, hour, 0, unroll=20)
     row = lax.broadcasted_iota(jnp.int32, (8, LANES), 0)
     lane8 = lax.broadcasted_iota(jnp.int32, (8, LANES), 1)
     lane = lax.broadcasted_iota(jnp.int32, (24, LANES), 1)

time: 108 us -> 107 us (level)
  no operation moved by 1% of the time
where the time goes in v5:
time: 107 us
  waiting for transfers between devices  48.5 us (45%)
  Pallas kernels  31.8 us (30%)
  starting transfers between devices  16.7 us (16%)
  local copies, waits for them, and re-layouts  9.46 us (9%)
    all_to_all x1, waiting for transfers between devices, on_device(): lax.all_to_all(field, ('x_hi', 'y'), split_axis=0, concat_axis=0, tiled=T...  35.2 us
    pallas_call x1, Pallas kernels, order_columns(): pl.pallas_call(order_kernel, grid=(rows // few,), in_specs=[pl.BlockSpec(...  14 us
    all_to_all x1, waiting for transfers between devices, on_device(): lax.all_to_all(blocks, ('core', 'z', 'y', 'x_hi', 'x_lo'), split_axis=0,...  13.3 us
    pallas_call x1, Pallas kernels, time_product(): pl.pallas_call(time_kernel, grid=(out_rows // few,), in_specs=[WHOLE, OUT...  10.8 us
    unnamed x8, local copies, waits for them, and re-layouts  9.39 us
    all_to_all x1, starting transfers between devices, on_device(): lax.all_to_all(blocks, ('core', 'z', 'y', 'x_hi', 'x_lo'), split_axis=0,...  9.05 us
    all_to_all x1, starting transfers between devices, on_device(): lax.all_to_all(field, ('x_hi', 'y'), split_axis=0, concat_axis=0, tiled=T...  7.61 us
    pallas_call x1, Pallas kernels, mix(): pl.pallas_call(mix_kernel, in_specs=[WHOLE] * 3, out_specs=OUTSIDE, out_s...  6.94 us
  transfers between devices with their start and end apart: 2, of which 2 were waited for; matrix products, arithmetic and copies ran while one was open for 0% of the time, Pallas kernels for 13%

profile of v5, /device:TPU:1, one launch (start us, length us, event | category | flops | bytes accessed | tf_op | source)
XLA Modules:
  0.0 106.8 jit_solution(5141370205657289794)
XLA Ops:
  0.0 0.0 copy-start.3
  0.0 0.0 copy-start.2
  0.0 7.6 %all-to-all-start = ((bf16[160,24,360]{2,1,0:T(8,128)(2,1)}), bf16[160,24,360]{2,1,0:T(8,128)(2,1)S(1)}, u32[]{:S(2)}, u32[]{:S(2)}) async-start(bf16[160,24,360]{2,1,0:T(8,128)(2,1)} %param.4), calls=%async_computation | async-start | bytes 5898240 | tf_op jit(solution)/shard_map/all_to_all | solution.py:260
  7.6 0.0 copy-done.3
  7.6 0.1 reshape.146
  7.7 35.2 %all-to-all-done = bf16[160,24,360]{2,1,0:T(8,128)(2,1)S(1)} async-done(((bf16[160,24,360]{2,1,0:T(8,128)(2,1)}), bf16[160,24,360]{2,1,0:T(8,128)(2,1)S(1)}, u32[]{:S(2)}, u32[]{:S(2)}) %all-to-all-start) | async-done | bytes 2764832 | tf_op jit(solution)/shard_map/all_to_all | solution.py:260
  42.9 0.0 copy-done.2
  42.9 6.9 %shard_map.46 = bf16[128,88,128]{2,1,0:T(8,128)(2,1)} custom-call(bf16[8,20,24,360]{3,2,1,0:T(8,128)(2,1)S(1)} %bitcast.4, bf16[360,360]{1,0:T(8,128)(2,1)S(1)} %copy-done.2, bf16[192,192]{1,0:T(8,128)(2,1)S(1)} %bitcast.5), custom_call_target="tpu_custom_call" | custom-call | tf_op jit(solution)/shard_map/pallas_call | solution.py:124
  49.8 9.1 %all-to-all-start.1 = ((bf16[128,88,128]{2,1,0:T(8,128)(2,1)}), bf16[128,88,128]{2,1,0:T(8,128)(2,1)S(1)}, u32[]{:S(2)}, u32[]{:S(2)}) async-start(bf16[128,88,128]{2,1,0:T(8,128)(2,1)} %shard_map.46), calls=%async_computation.1 | async-start | bytes 5767168 | tf_op jit(solution)/shard_map/all_to_all | solution.py:264
  58.9 0.3 fusion.move_ref
  59.2 0.0 copy-start.1
  59.2 4.7 %copy-done.1 = bf16[2560,2560]{1,0:T(8,128)(2,1)S(1)} copy-done((bf16[2560,2560]{1,0:T(8,128)(2,1)S(1)}, bf16[2560,2560]{1,0:T(8,128)(2,1)}, u32[]{:S(2)}) %copy-start.1) | copy-done | bytes 13107224
  63.9 14.0 %shard_map.47.t_ref = bf16[2560,2560]{1,0:T(8,128)(2,1)S(1)} custom-call(bf16[2560,2560]{1,0:T(8,128)(2,1)S(1)} %copy-done.1, bf16[640,640]{1,0:T(8,128)(2,1)S(1)} %fusion.move_ref), custom_call_target="tpu_custom_call" | custom-call | tf_op jit(solution)/shard_map/pallas_call | solution.py:173
  78.0 0.0 copy-start
  78.0 4.7 %copy-done = bf16[2560,2560]{1,0:T(8,128)(2,1)} copy-done((bf16[2560,2560]{1,0:T(8,128)(2,1)}, bf16[2560,2560]{1,0:T(8,128)(2,1)S(1)}, u32[]{:S(2)}) %copy-start) | copy-done | bytes 13107224
  82.6 13.3 %all-to-all-done.1.r_ref = bf16[128,88,128]{2,1,0:T(8,128)(2,1)S(1)} async-done(((bf16[128,88,128]{2,1,0:T(8,128)(2,1)}), bf16[128,88,128]{2,1,0:T(8,128)(2,1)S(1)}, u32[]{:S(2)}, u32[]{:S(2)}) %all-to-all-start.1) | async-done | bytes 2883616 | tf_op jit(solution)/shard_map/all_to_all | solution.py:264
  96.0 10.8 %shard_map.48 = bf16[540,2560]{1,0:T(8,128)(2,1)} custom-call(bf16[128,88,128]{2,1,0:T(8,128)(2,1)S(1)} %all-to-all-done.1.r_ref, bf16[2560,2560]{1,0:T(8,128)(2,1)} %copy-done), custom_call_target="tpu_custom_call" | custom-call | tf_op jit(solution)/shard_map/pallas_call | solution.py:236
  (2 shorter events, 0.1 us)
Async XLA Ops:
  0.0 7.6 %copy-start.3 = (bf16[192,192]{1,0:T(8,128)(2,1)S(1)}, bf16[192,192]{1,0:T(8,128)(2,1)}, u32[]{:S(2)}) copy-start(bf16[192,192]{1,0:T(8,128)(2,1)} %param.6) | copy-start | bytes 221188
  0.0 42.9 %copy-start.2 = (bf16[360,360]{1,0:T(8,128)(2,1)S(1)}, bf16[360,360]{1,0:T(8,128)(2,1)}, u32[]{:S(2)}) copy-start(bf16[360,360]{1,0:T(8,128)(2,1)} %lon_ref.1) | copy-start | bytes 777604
  0.0 42.9 %all-to-all-start = ((bf16[160,24,360]{2,1,0:T(8,128)(2,1)}), bf16[160,24,360]{2,1,0:T(8,128)(2,1)S(1)}, u32[]{:S(2)}, u32[]{:S(2)}) async-start(bf16[160,24,360]{2,1,0:T(8,128)(2,1)} %param.4), calls=%async_computation | async-start | bytes 5898240 | tf_op jit(solution)/shard_map/all_to_all | solution.py:260
  49.8 46.1 %all-to-all-start.1 = ((bf16[128,88,128]{2,1,0:T(8,128)(2,1)}), bf16[128,88,128]{2,1,0:T(8,128)(2,1)S(1)}, u32[]{:S(2)}, u32[]{:S(2)}) async-start(bf16[128,88,128]{2,1,0:T(8,128)(2,1)} %shard_map.46), calls=%async_computation.1 | async-start | bytes 5767168 | tf_op jit(solution)/shard_map/all_to_all | solution.py:264
  59.2 4.7 %copy-start.1 = (bf16[2560,2560]{1,0:T(8,128)(2,1)S(1)}, bf16[2560,2560]{1,0:T(8,128)(2,1)}, u32[]{:S(2)}) copy-start(bf16[2560,2560]{1,0:T(8,128)(2,1)} %t_ref.1) | copy-start | bytes 39321604
  78.0 4.7 %copy-start = (bf16[2560,2560]{1,0:T(8,128)(2,1)}, bf16[2560,2560]{1,0:T(8,128)(2,1)S(1)}, u32[]{:S(2)}) copy-start(bf16[2560,2560]{1,0:T(8,128)(2,1)S(1)} %shard_map.47.t_ref) | copy-start | bytes 39321604

commit v6 on v5

--- a/solution.py
+++ b/solution.py
@@ -141,20 +141,19 @@
     total = t_ref.shape[1]
     groups = total // GROUP
     main, tail = 16 * MAIN, 16 * (HOURS - MAIN)
-    tails = []
+    start = 2 * groups * main
     for z in range(groups):
-        w = jnp.dot(t_ref[:, GROUP * z : GROUP * (z + 1)], move, preferred_element_type=jnp.float32)
+        w = lax.dot_general(
+            move,
+            t_ref[:, GROUP * z : GROUP * (z + 1)],
+            (((0,), (1,)), ((), ())),
+            preferred_element_type=jnp.float32,
+        ).astype(jnp.bfloat16)
         for core in range(2):
             at = (core * groups + z) * main
-            out_ref[:, at : at + main] = w[:, main * core : main * (core + 1)].astype(jnp.bfloat16)
-        tails.append(w[:, 2 * main :])
-    low = lax.broadcasted_iota(jnp.int32, tails[0].shape, 1) < tail
-    start = 2 * groups * main
-    for z in range(0, groups, 2):
-        x, y = tails[z], tails[z + 1]
-        for core, both in enumerate((jnp.where(low, x, pltpu.roll(y, tail, 1)), jnp.where(low, pltpu.roll(x, tail, 1), y))):
+            out_ref[at : at + main, :] = w[main * core : main * (core + 1)]
             at = start + (core * groups + z) * tail
-            out_ref[:, at : at + 2 * tail] = both.astype(jnp.bfloat16)
+            out_ref[at : at + tail, :] = w[2 * main + tail * core : 2 * main + tail * (core + 1)]
 
 
 def order_columns(time_factor):
@@ -174,8 +173,8 @@
         order_kernel,
         grid=(rows // few,),
         in_specs=[pl.BlockSpec((few, total), lambda i: (i, 0)), pl.BlockSpec((GROUP, GROUP), lambda i: (0, 0))],
-        out_specs=pl.BlockSpec((few, total), lambda i: (i, 0)),
-        out_shape=jax.ShapeDtypeStruct((rows, total), jnp.bfloat16),
+        out_specs=pl.BlockSpec((total, few), lambda i: (0, i)),
+        out_shape=jax.ShapeDtypeStruct((total, rows), jnp.bfloat16),
         compiler_params=params(16),
     )(time_factor, move)
 
@@ -212,7 +211,7 @@
 
     def arrival(n):
         at = pl.ds(pl.multiple_of(n * few, few), few)
-        return pltpu.make_async_copy(t_ref.at[at], held_ref.at[at], sem.at[n])
+        return pltpu.make_async_copy(t_ref.at[:, at], held_ref.at[n], sem.at[n])
 
     @pl.when(step == 0)
     def _():
@@ -225,14 +224,13 @@
         arrival(step + 2).start()
 
     arrival(step).wait()
-    t = held_ref[pl.ds(pl.multiple_of(step * few, few), few), :]
-    w = lax.dot_general(gt_ref[...], t, (((1,), (1,)), ((), ())), preferred_element_type=jnp.float32)
+    w = jnp.dot(gt_ref[...], held_ref[step], preferred_element_type=jnp.float32)
     out_ref[...] = w[:CELLS].astype(jnp.bfloat16)
 
 
 def time_product(r, t):
     few = 512
-    out_rows, total = t.shape
+    total, out_rows = t.shape
     return pl.pallas_call(
         time_kernel,
         grid=(out_rows // few,),
@@ -242,7 +240,7 @@
         scratch_shapes=[
             pltpu.VMEM((TALL, total), jnp.bfloat16),
             pltpu.VMEM((r.shape[0] * (BLOCK - 64), LANES), jnp.float32),
-            pltpu.VMEM((out_rows, total), jnp.bfloat16),
+            pltpu.VMEM((out_rows // few, total, few), jnp.bfloat16),
             pltpu.SemaphoreType.DMA((out_rows // few,)),
         ],
         compiler_params=params(40),

time: 107 us -> 107 us (level)
  transfers between devices with their start and end apart: 2 -> 2, of which waited for: 2 -> 2; matrix products, arithmetic and copies ran while one was open for 0% -> 0% of each run, Pallas kernels for 13% -> 12%
where the time goes in v6:
time: 107 us
  waiting for transfers between devices  49.4 us (46%)
  Pallas kernels  30.8 us (29%)
  starting transfers between devices  16.7 us (16%)
  local copies, waits for them, and re-layouts  9.46 us (9%)
    all_to_all x1, waiting for transfers between devices, on_device(): lax.all_to_all(field, ('x_hi', 'y'), split_axis=0, concat_axis=0, tiled=T...  35.2 us
    all_to_all x1, waiting for transfers between devices, on_device(): lax.all_to_all(blocks, ('core', 'z', 'y', 'x_hi', 'x_lo'), split_axis=0,...  14.2 us
    pallas_call x1, Pallas kernels, order_columns(): pl.pallas_call(order_kernel, grid=(rows // few,), in_specs=[pl.BlockSpec(...  13.1 us
    pallas_call x1, Pallas kernels, time_product(): pl.pallas_call(time_kernel, grid=(out_rows // few,), in_specs=[WHOLE, OUT...  10.7 us
    unnamed x8, local copies, waits for them, and re-layouts  9.39 us
    all_to_all x1, starting transfers between devices, on_device(): lax.all_to_all(blocks, ('core', 'z', 'y', 'x_hi', 'x_lo'), split_axis=0,...  9.05 us
    all_to_all x1, starting transfers between devices, on_device(): lax.all_to_all(field, ('x_hi', 'y'), split_axis=0, concat_axis=0, tiled=T...  7.61 us
    pallas_call x1, Pallas kernels, mix(): pl.pallas_call(mix_kernel, in_specs=[WHOLE] * 3, out_specs=OUTSIDE, out_s...  6.94 us
  transfers between devices with their start and end apart: 2, of which 2 were waited for; matrix products, arithmetic and copies ran while one was open for 0% of the time, Pallas kernels for 12%

profile of v6, /device:TPU:1, one launch (start us, length us, event | category | flops | bytes accessed | tf_op | source)
XLA Modules:
  0.0 106.7 jit_solution(7168750332031622976)
XLA Ops:
  0.0 0.0 copy-start.3
  0.0 0.0 copy-start.2
  0.0 7.6 %all-to-all-start = ((bf16[160,24,360]{2,1,0:T(8,128)(2,1)}), bf16[160,24,360]{2,1,0:T(8,128)(2,1)S(1)}, u32[]{:S(2)}, u32[]{:S(2)}) async-start(bf16[160,24,360]{2,1,0:T(8,128)(2,1)} %param.4), calls=%async_computation | async-start | bytes 5898240 | tf_op jit(solution)/shard_map/all_to_all | solution.py:258
  7.6 0.0 copy-done.3
  7.6 0.1 reshape.146
  7.7 35.2 %all-to-all-done = bf16[160,24,360]{2,1,0:T(8,128)(2,1)S(1)} async-done(((bf16[160,24,360]{2,1,0:T(8,128)(2,1)}), bf16[160,24,360]{2,1,0:T(8,128)(2,1)S(1)}, u32[]{:S(2)}, u32[]{:S(2)}) %all-to-all-start) | async-done | bytes 2764832 | tf_op jit(solution)/shard_map/all_to_all | solution.py:258
  42.9 0.0 copy-done.2
  42.9 6.9 %shard_map.46 = bf16[128,88,128]{2,1,0:T(8,128)(2,1)} custom-call(bf16[8,20,24,360]{3,2,1,0:T(8,128)(2,1)S(1)} %bitcast.4, bf16[360,360]{1,0:T(8,128)(2,1)S(1)} %copy-done.2, bf16[192,192]{1,0:T(8,128)(2,1)S(1)} %bitcast.5), custom_call_target="tpu_custom_call" | custom-call | tf_op jit(solution)/shard_map/pallas_call | solution.py:124
  49.8 9.1 %all-to-all-start.1 = ((bf16[128,88,128]{2,1,0:T(8,128)(2,1)}), bf16[128,88,128]{2,1,0:T(8,128)(2,1)S(1)}, u32[]{:S(2)}, u32[]{:S(2)}) async-start(bf16[128,88,128]{2,1,0:T(8,128)(2,1)} %shard_map.46), calls=%async_computation.1 | async-start | bytes 5767168 | tf_op jit(solution)/shard_map/all_to_all | solution.py:262
  58.9 0.3 fusion.move_ref
  59.2 0.0 copy-start.1
  59.2 4.7 %copy-done.1 = bf16[2560,2560]{1,0:T(8,128)(2,1)S(1)} copy-done((bf16[2560,2560]{1,0:T(8,128)(2,1)S(1)}, bf16[2560,2560]{1,0:T(8,128)(2,1)}, u32[]{:S(2)}) %copy-start.1) | copy-done | bytes 13107224
  63.9 13.1 %shard_map.47.t_ref = bf16[2560,2560]{1,0:T(8,128)(2,1)S(1)} custom-call(bf16[2560,2560]{1,0:T(8,128)(2,1)S(1)} %copy-done.1, bf16[640,640]{1,0:T(8,128)(2,1)S(1)} %fusion.move_ref), custom_call_target="tpu_custom_call" | custom-call | tf_op jit(solution)/shard_map/pallas_call | solution.py:172
  77.1 0.0 copy-start
  77.1 4.7 %copy-done = bf16[2560,2560]{1,0:T(8,128)(2,1)} copy-done((bf16[2560,2560]{1,0:T(8,128)(2,1)}, bf16[2560,2560]{1,0:T(8,128)(2,1)S(1)}, u32[]{:S(2)}) %copy-start) | copy-done | bytes 13107224
  81.8 14.2 %all-to-all-done.1.r_ref = bf16[128,88,128]{2,1,0:T(8,128)(2,1)S(1)} async-done(((bf16[128,88,128]{2,1,0:T(8,128)(2,1)}), bf16[128,88,128]{2,1,0:T(8,128)(2,1)S(1)}, u32[]{:S(2)}, u32[]{:S(2)}) %all-to-all-start.1) | async-done | bytes 2883616 | tf_op jit(solution)/shard_map/all_to_all | solution.py:262
  96.0 10.7 %shard_map.48 = bf16[540,2560]{1,0:T(8,128)(2,1)} custom-call(bf16[128,88,128]{2,1,0:T(8,128)(2,1)S(1)} %all-to-all-done.1.r_ref, bf16[2560,2560]{1,0:T(8,128)(2,1)} %copy-done), custom_call_target="tpu_custom_call" | custom-call | tf_op jit(solution)/shard_map/pallas_call | solution.py:234
  (2 shorter events, 0.1 us)
Async XLA Ops:
  0.0 7.6 %copy-start.3 = (bf16[192,192]{1,0:T(8,128)(2,1)S(1)}, bf16[192,192]{1,0:T(8,128)(2,1)}, u32[]{:S(2)}) copy-start(bf16[192,192]{1,0:T(8,128)(2,1)} %param.6) | copy-start | bytes 221188
  0.0 42.9 %copy-start.2 = (bf16[360,360]{1,0:T(8,128)(2,1)S(1)}, bf16[360,360]{1,0:T(8,128)(2,1)}, u32[]{:S(2)}) copy-start(bf16[360,360]{1,0:T(8,128)(2,1)} %lon_ref.1) | copy-start | bytes 777604
  0.0 42.9 %all-to-all-start = ((bf16[160,24,360]{2,1,0:T(8,128)(2,1)}), bf16[160,24,360]{2,1,0:T(8,128)(2,1)S(1)}, u32[]{:S(2)}, u32[]{:S(2)}) async-start(bf16[160,24,360]{2,1,0:T(8,128)(2,1)} %param.4), calls=%async_computation | async-start | bytes 5898240 | tf_op jit(solution)/shard_map/all_to_all | solution.py:258
  49.8 46.1 %all-to-all-start.1 = ((bf16[128,88,128]{2,1,0:T(8,128)(2,1)}), bf16[128,88,128]{2,1,0:T(8,128)(2,1)S(1)}, u32[]{:S(2)}, u32[]{:S(2)}) async-start(bf16[128,88,128]{2,1,0:T(8,128)(2,1)} %shard_map.46), calls=%async_computation.1 | async-start | bytes 5767168 | tf_op jit(solution)/shard_map/all_to_all | solution.py:262
  59.2 4.7 %copy-start.1 = (bf16[2560,2560]{1,0:T(8,128)(2,1)S(1)}, bf16[2560,2560]{1,0:T(8,128)(2,1)}, u32[]{:S(2)}) copy-start(bf16[2560,2560]{1,0:T(8,128)(2,1)} %t_ref.1) | copy-start | bytes 39321604
  77.1 4.7 %copy-start = (bf16[2560,2560]{1,0:T(8,128)(2,1)}, bf16[2560,2560]{1,0:T(8,128)(2,1)S(1)}, u32[]{:S(2)}) copy-start(bf16[2560,2560]{1,0:T(8,128)(2,1)S(1)} %shard_map.47.t_ref) | copy-start | bytes 39321604

commit v7 on v6

--- a/solution.py
+++ b/solution.py
@@ -258,6 +258,7 @@
     moved = lax.all_to_all(field, ("x_hi", "y"), split_axis=0, concat_axis=0, tiled=True)
     ordered = order_columns(time_factor)
     lat = by_thirds(lat_factor)
+    moved, ordered = lax.optimization_barrier((moved, ordered))
     blocks = mix(moved.reshape(parts, hours // parts, few, columns), lon_factor, lat)
     got = lax.all_to_all(blocks, ("core", "z", "y", "x_hi", "x_lo"), split_axis=0, concat_axis=0, tiled=True)
     return time_product(got, ordered).T

time: 107 us -> 107 us (level)
  blocking collectives: 0 us -> 46.1 us
  waiting for transfers between devices: 49.4 us -> 12.3 us
  starting transfers between devices: 16.7 us -> 7.61 us
    all_to_all x0 -> x1, blocking collectives: none -> 46.1 us  [on_device(): lax.all_to_all(blocks, ('core', 'z', 'y', 'x_hi', 'x_lo'), split_axis=0,...]
    all_to_all x1, waiting for transfers between devices: 35.2 us -> 12.3 us  [on_device(): lax.all_to_all(field, ('x_hi', 'y'), split_axis=0, concat_axis=0, tiled=T...]
    all_to_all x1 -> x0, waiting for transfers between devices: 14.2 us -> none  [on_device(): lax.all_to_all(blocks, ('core', 'z', 'y', 'x_hi', 'x_lo'), split_axis=0,...]
    all_to_all x1 -> x0, starting transfers between devices: 9.05 us -> none  [on_device(): lax.all_to_all(blocks, ('core', 'z', 'y', 'x_hi', 'x_lo'), split_axis=0,...]
  transfers between devices with their start and end apart: 2 -> 1, of which waited for: 2 -> 1; matrix products, arithmetic and copies ran while one was open for 0% -> 0% of each run, Pallas kernels for 12% -> 12%
where the time goes in v7:
time: 107 us
  blocking collectives  46.1 us (43%)
  Pallas kernels  30.8 us (29%)
  waiting for transfers between devices  12.3 us (11%)
  local copies, waits for them, and re-layouts  9.46 us (9%)
  starting transfers between devices  7.61 us (7%)
    all_to_all x1, blocking collectives, on_device(): lax.all_to_all(blocks, ('core', 'z', 'y', 'x_hi', 'x_lo'), split_axis=0,...  46.1 us
    pallas_call x1, Pallas kernels, order_columns(): pl.pallas_call(order_kernel, grid=(rows // few,), in_specs=[pl.BlockSpec(...  13.1 us
    all_to_all x1, waiting for transfers between devices, on_device(): lax.all_to_all(field, ('x_hi', 'y'), split_axis=0, concat_axis=0, tiled=T...  12.3 us
    pallas_call x1, Pallas kernels, time_product(): pl.pallas_call(time_kernel, grid=(out_rows // few,), in_specs=[WHOLE, OUT...  10.7 us
    unnamed x8, local copies, waits for them, and re-layouts  9.39 us
    all_to_all x1, starting transfers between devices, on_device(): lax.all_to_all(field, ('x_hi', 'y'), split_axis=0, concat_axis=0, tiled=T...  7.61 us
    pallas_call x1, Pallas kernels, mix(): pl.pallas_call(mix_kernel, in_specs=[WHOLE] * 3, out_specs=OUTSIDE, out_s...  6.94 us
  transfers between devices with their start and end apart: 1, of which 1 were waited for; matrix products, arithmetic and copies ran while one was open for 0% of the time, Pallas kernels for 12%

profile of v7, /device:TPU:1, one launch (start us, length us, event | category | flops | bytes accessed | tf_op | source)
XLA Modules:
  0.0 106.7 jit_solution(14629365157852592950)
XLA Ops:
  0.0 0.0 copy-start.3
  0.0 7.6 %all-to-all-start = ((bf16[160,24,360]{2,1,0:T(8,128)(2,1)}), bf16[160,24,360]{2,1,0:T(8,128)(2,1)S(1)}, u32[]{:S(2)}, u32[]{:S(2)}) async-start(bf16[160,24,360]{2,1,0:T(8,128)(2,1)} %param.4), calls=%async_computation | async-start | bytes 5898240 | tf_op jit(solution)/shard_map/all_to_all | solution.py:258
  7.6 0.0 copy-done.3
  7.6 0.1 reshape.146
  7.7 0.3 fusion.move_ref
  8.0 0.0 copy-start.1
  8.0 4.7 %copy-done.1 = bf16[2560,2560]{1,0:T(8,128)(2,1)S(1)} copy-done((bf16[2560,2560]{1,0:T(8,128)(2,1)S(1)}, bf16[2560,2560]{1,0:T(8,128)(2,1)}, u32[]{:S(2)}) %copy-start.1) | copy-done | bytes 13107224
  12.7 0.0 copy-start.2
  12.7 13.1 %shard_map.46.t_ref = bf16[2560,2560]{1,0:T(8,128)(2,1)S(1)} custom-call(bf16[2560,2560]{1,0:T(8,128)(2,1)S(1)} %copy-done.1, bf16[640,640]{1,0:T(8,128)(2,1)S(1)} %fusion.move_ref), custom_call_target="tpu_custom_call" | custom-call | tf_op jit(solution)/shard_map/pallas_call | solution.py:172
  25.9 0.0 copy-start
  25.9 4.7 %copy-done = bf16[2560,2560]{1,0:T(8,128)(2,1)} copy-done((bf16[2560,2560]{1,0:T(8,128)(2,1)}, bf16[2560,2560]{1,0:T(8,128)(2,1)S(1)}, u32[]{:S(2)}) %copy-start) | copy-done | bytes 13107224
  30.6 12.3 %all-to-all-done = bf16[160,24,360]{2,1,0:T(8,128)(2,1)S(1)} async-done(((bf16[160,24,360]{2,1,0:T(8,128)(2,1)}), bf16[160,24,360]{2,1,0:T(8,128)(2,1)S(1)}, u32[]{:S(2)}, u32[]{:S(2)}) %all-to-all-start) | async-done | bytes 2764832 | tf_op jit(solution)/shard_map/all_to_all | solution.py:258
  42.9 0.0 copy-done.2
  42.9 6.9 %shard_map.47 = bf16[128,88,128]{2,1,0:T(8,128)(2,1)} custom-call(bf16[8,20,24,360]{3,2,1,0:T(8,128)(2,1)S(1)} %bitcast.4, bf16[360,360]{1,0:T(8,128)(2,1)S(1)} %copy-done.2, bf16[192,192]{1,0:T(8,128)(2,1)S(1)} %bitcast.5), custom_call_target="tpu_custom_call" | custom-call | tf_op jit(solution)/shard_map/pallas_call | solution.py:124
  49.8 46.1 %all_to_all.10.r_ref = bf16[128,88,128]{2,1,0:T(8,128)(2,1)S(1)} all-to-all(bf16[128,88,128]{2,1,0:T(8,128)(2,1)} %shard_map.47), channel_id=1, replica_groups=mesh['z'=4,'x_lo'=2,'core'=2,'x_hi'=2,'y'=4] {'core','z','y','x_hi','x_lo'}, dimensions={0} | all-to-all | bytes 5767168 | tf_op jit(solution)/shard_map/all_to_all | solution.py:263
  96.0 10.7 %shard_map.48 = bf16[540,2560]{1,0:T(8,128)(2,1)} custom-call(bf16[128,88,128]{2,1,0:T(8,128)(2,1)S(1)} %all_to_all.10.r_ref, bf16[2560,2560]{1,0:T(8,128)(2,1)} %copy-done), custom_call_target="tpu_custom_call" | custom-call | tf_op jit(solution)/shard_map/pallas_call | solution.py:234
  (2 shorter events, 0.1 us)
Async XLA Ops:
  0.0 7.6 %copy-start.3 = (bf16[192,192]{1,0:T(8,128)(2,1)S(1)}, bf16[192,192]{1,0:T(8,128)(2,1)}, u32[]{:S(2)}) copy-start(bf16[192,192]{1,0:T(8,128)(2,1)} %param.6) | copy-start | bytes 221188
  0.0 42.9 %all-to-all-start = ((bf16[160,24,360]{2,1,0:T(8,128)(2,1)}), bf16[160,24,360]{2,1,0:T(8,128)(2,1)S(1)}, u32[]{:S(2)}, u32[]{:S(2)}) async-start(bf16[160,24,360]{2,1,0:T(8,128)(2,1)} %param.4), calls=%async_computation | async-start | bytes 5898240 | tf_op jit(solution)/shard_map/all_to_all | solution.py:258
  8.0 4.7 %copy-start.1 = (bf16[2560,2560]{1,0:T(8,128)(2,1)S(1)}, bf16[2560,2560]{1,0:T(8,128)(2,1)}, u32[]{:S(2)}) copy-start(bf16[2560,2560]{1,0:T(8,128)(2,1)} %t_ref.1) | copy-start | bytes 39321604
  12.7 30.2 %copy-start.2 = (bf16[360,360]{1,0:T(8,128)(2,1)S(1)}, bf16[360,360]{1,0:T(8,128)(2,1)}, u32[]{:S(2)}) copy-start(bf16[360,360]{1,0:T(8,128)(2,1)} %lon_ref.1) | copy-start | bytes 777604
  25.9 4.7 %copy-start = (bf16[2560,2560]{1,0:T(8,128)(2,1)}, bf16[2560,2560]{1,0:T(8,128)(2,1)S(1)}, u32[]{:S(2)}) copy-start(bf16[2560,2560]{1,0:T(8,128)(2,1)S(1)} %shard_map.46.t_ref) | copy-start | bytes 39321604

commit v8 on v7

--- a/solution.py
+++ b/solution.py
@@ -174,7 +174,7 @@
         grid=(rows // few,),
         in_specs=[pl.BlockSpec((few, total), lambda i: (i, 0)), pl.BlockSpec((GROUP, GROUP), lambda i: (0, 0))],
         out_specs=pl.BlockSpec((total, few), lambda i: (0, i)),
-        out_shape=jax.ShapeDtypeStruct((total, rows), jnp.bfloat16),
+        out_shape=pltpu.HBM((total, rows), jnp.bfloat16),
         compiler_params=params(16),
     )(time_factor, move)
 

time: 107 us -> 107 us (level)
  local copies, waits for them, and re-layouts: 9.46 us -> 4.8 us
  waiting for transfers between devices: 12.3 us -> 16.6 us
    unnamed x8 -> x6, local copies, waits for them, and re-layouts: 9.39 us -> 4.73 us
    all_to_all x1, waiting for transfers between devices: 12.3 us -> 16.6 us  [on_device(): lax.all_to_all(field, ('x_hi', 'y'), split_axis=0, concat_axis=0, tiled=T...]
  transfers between devices with their start and end apart: 1 -> 1, of which waited for: 1 -> 1; matrix products, arithmetic and copies ran while one was open for 0% -> 0% of each run, Pallas kernels for 12% -> 13%
where the time goes in v8:
time: 107 us
  blocking collectives  46.1 us (43%)
  Pallas kernels  31.2 us (29%)
  waiting for transfers between devices  16.6 us (16%)
  starting transfers between devices  7.61 us (7%)
  local copies, waits for them, and re-layouts  4.8 us (4%)
    all_to_all x1, blocking collectives, on_device(): lax.all_to_all(blocks, ('core', 'z', 'y', 'x_hi', 'x_lo'), split_axis=0,...  46.1 us
    all_to_all x1, waiting for transfers between devices, on_device(): lax.all_to_all(field, ('x_hi', 'y'), split_axis=0, concat_axis=0, tiled=T...  16.6 us
    pallas_call x1, Pallas kernels, order_columns(): pl.pallas_call(order_kernel, grid=(rows // few,), in_specs=[pl.BlockSpec(...  13.6 us
    pallas_call x1, Pallas kernels, time_product(): pl.pallas_call(time_kernel, grid=(out_rows // few,), in_specs=[WHOLE, OUT...  10.7 us
    all_to_all x1, starting transfers between devices, on_device(): lax.all_to_all(field, ('x_hi', 'y'), split_axis=0, concat_axis=0, tiled=T...  7.61 us
    pallas_call x1, Pallas kernels, mix(): pl.pallas_call(mix_kernel, in_specs=[WHOLE] * 3, out_specs=OUTSIDE, out_s...  6.94 us
    unnamed x6, local copies, waits for them, and re-layouts  4.73 us
  transfers between devices with their start and end apart: 1, of which 1 were waited for; matrix products, arithmetic and copies ran while one was open for 0% of the time, Pallas kernels for 13%

profile of v8, /device:TPU:1, one launch (start us, length us, event | category | flops | bytes accessed | tf_op | source)
XLA Modules:
  0.0 106.7 jit_solution(7487896169105987698)
XLA Ops:
  0.0 0.0 copy-start.2
  0.0 7.6 %all-to-all-start = ((bf16[160,24,360]{2,1,0:T(8,128)(2,1)}), bf16[160,24,360]{2,1,0:T(8,128)(2,1)S(1)}, u32[]{:S(2)}, u32[]{:S(2)}) async-start(bf16[160,24,360]{2,1,0:T(8,128)(2,1)} %param.4), calls=%async_computation | async-start | bytes 5898240 | tf_op jit(solution)/shard_map/all_to_all | solution.py:258
  7.6 0.0 copy-done.2
  7.6 0.1 reshape.146
  7.7 0.3 fusion.move_ref
  8.0 0.0 copy-start
  8.0 4.7 %copy-done = bf16[2560,2560]{1,0:T(8,128)(2,1)S(1)} copy-done((bf16[2560,2560]{1,0:T(8,128)(2,1)S(1)}, bf16[2560,2560]{1,0:T(8,128)(2,1)}, u32[]{:S(2)}) %copy-start) | copy-done | bytes 13107224
  12.7 0.0 copy-start.1
  12.7 13.6 %shard_map.46.t_ref = bf16[2560,2560]{1,0:T(8,128)(2,1)} custom-call(bf16[2560,2560]{1,0:T(8,128)(2,1)S(1)} %copy-done, bf16[640,640]{1,0:T(8,128)(2,1)S(1)} %fusion.move_ref), custom_call_target="tpu_custom_call" | custom-call | tf_op jit(solution)/shard_map/pallas_call | solution.py:172
  26.3 16.6 %all-to-all-done = bf16[160,24,360]{2,1,0:T(8,128)(2,1)S(1)} async-done(((bf16[160,24,360]{2,1,0:T(8,128)(2,1)}), bf16[160,24,360]{2,1,0:T(8,128)(2,1)S(1)}, u32[]{:S(2)}, u32[]{:S(2)}) %all-to-all-start) | async-done | bytes 2764832 | tf_op jit(solution)/shard_map/all_to_all | solution.py:258
  42.9 0.0 copy-done.1
  42.9 6.9 %shard_map.47 = bf16[128,88,128]{2,1,0:T(8,128)(2,1)} custom-call(bf16[8,20,24,360]{3,2,1,0:T(8,128)(2,1)S(1)} %bitcast.4, bf16[360,360]{1,0:T(8,128)(2,1)S(1)} %copy-done.1, bf16[192,192]{1,0:T(8,128)(2,1)S(1)} %bitcast.5), custom_call_target="tpu_custom_call" | custom-call | tf_op jit(solution)/shard_map/pallas_call | solution.py:124
  49.8 46.1 %all_to_all.10.r_ref = bf16[128,88,128]{2,1,0:T(8,128)(2,1)S(1)} all-to-all(bf16[128,88,128]{2,1,0:T(8,128)(2,1)} %shard_map.47), channel_id=1, replica_groups=mesh['z'=4,'x_lo'=2,'core'=2,'x_hi'=2,'y'=4] {'core','z','y','x_hi','x_lo'}, dimensions={0} | all-to-all | bytes 5767168 | tf_op jit(solution)/shard_map/all_to_all | solution.py:263
  96.0 10.7 %shard_map.48 = bf16[540,2560]{1,0:T(8,128)(2,1)} custom-call(bf16[128,88,128]{2,1,0:T(8,128)(2,1)S(1)} %all_to_all.10.r_ref, bf16[2560,2560]{1,0:T(8,128)(2,1)} %shard_map.46.t_ref), custom_call_target="tpu_custom_call" | custom-call | tf_op jit(solution)/shard_map/pallas_call | solution.py:234
  (2 shorter events, 0.1 us)
Async XLA Ops:
  0.0 7.6 %copy-start.2 = (bf16[192,192]{1,0:T(8,128)(2,1)S(1)}, bf16[192,192]{1,0:T(8,128)(2,1)}, u32[]{:S(2)}) copy-start(bf16[192,192]{1,0:T(8,128)(2,1)} %param.6) | copy-start | bytes 221188
  0.0 42.9 %all-to-all-start = ((bf16[160,24,360]{2,1,0:T(8,128)(2,1)}), bf16[160,24,360]{2,1,0:T(8,128)(2,1)S(1)}, u32[]{:S(2)}, u32[]{:S(2)}) async-start(bf16[160,24,360]{2,1,0:T(8,128)(2,1)} %param.4), calls=%async_computation | async-start | bytes 5898240 | tf_op jit(solution)/shard_map/all_to_all | solution.py:258
  8.0 4.7 %copy-start = (bf16[2560,2560]{1,0:T(8,128)(2,1)S(1)}, bf16[2560,2560]{1,0:T(8,128)(2,1)}, u32[]{:S(2)}) copy-start(bf16[2560,2560]{1,0:T(8,128)(2,1)} %t_ref.1) | copy-start | bytes 39321604
  12.7 30.2 %copy-start.1 = (bf16[360,360]{1,0:T(8,128)(2,1)S(1)}, bf16[360,360]{1,0:T(8,128)(2,1)}, u32[]{:S(2)}) copy-start(bf16[360,360]{1,0:T(8,128)(2,1)} %lon_ref.1) | copy-start | bytes 777604
